TPU v7x, 32 devices: a whole 2x2x4 slice. The times are simulated.
32 devices in a mesh: dp: 8 (over z, x), tensor: 4 (over y, core).
Axes of the slice: x: 2, y: 2, z: 4, core: 2. Of those that a mesh axis runs over, the one named last changes fastest.
Arguments:
- activations: bfloat16 [2048, 4096], P('dp'), may hold values from -6 to 6
- grad_output: bfloat16 [2048, 14336], P('dp', 'tensor'), may hold values from -6 to 6
- weight: bfloat16 [4096, 14336], P('dp', 'tensor'), may hold values from -0.09375 to 0.09375
- start_basis: float32 [14336, 64], P('tensor'), may hold values from -6 to 6
Outputs:
- input_grad: bfloat16 [2048, 4096], P('dp', 'tensor')
- right_basis: float32 [14336, 64], P('tensor')
- new_weight: float32 [4096, 14336], P('dp', 'tensor')
All inputs are finite; a program needn't handle non-finite values.
Results may differ from a plain program's by a relative error of at most 0.018.
Values may be sent and summed in bfloat16 or wider, within the bound.
A program may use at most 128 MiB of HBM per device.

v0:
```python
import jax
import jax.numpy as jnp
from jax import lax
from jax.sharding import PartitionSpec as P

learn_rate = 0.001


def orthonormal_basis(left):
    gram_matrix = jnp.dot(left.T, left, precision=lax.Precision.HIGHEST)
    lower = jnp.linalg.cholesky(gram_matrix)
    return lower


def split_parts(values):
    upper_part = values.astype(jnp.bfloat16)
    lower_part = (values - upper_part.astype(jnp.float32)).astype(jnp.bfloat16)
    return (upper_part, lower_part)


def thin_product(wide, thin_values, dims):
    upper_part, lower_part = split_parts(thin_values)
    first = lax.dot_general(wide, upper_part, dims, preferred_element_type=jnp.float32)
    second = lax.dot_general(wide, lower_part, dims, preferred_element_type=jnp.float32)
    return first + second


def body(activations, grad_output, weight, start_basis):
    partial_input = lax.dot_general(
        grad_output,
        lax.all_gather(weight, "dp", axis=0, tiled=True),
        (((1,), (1,)), ((), ())),
        preferred_element_type=jnp.float32,
    )
    input_grad = lax.psum_scatter(
        partial_input.astype(jnp.bfloat16), "tensor", scatter_dimension=1, tiled=True
    )
    plain_dims = (((1,), (0,)), ((), ()))
    token_dims = (((0,), (0,)), ((), ()))
    thin_rows = thin_product(grad_output, start_basis, plain_dims)
    left_part = thin_product(activations, thin_rows, token_dims)
    left = lax.psum(left_part, ("dp", "tensor"))
    lower = orthonormal_basis(left)
    left_basis = jax.scipy.linalg.solve_triangular(lower, left.T, lower=True).T
    token_proj = thin_product(activations, left_basis, plain_dims)
    right_part = thin_product(grad_output, token_proj, token_dims)
    right = lax.psum(right_part.astype(jnp.bfloat16), "dp").astype(jnp.float32)
    token_total = activations.shape[0] * lax.axis_size("dp")
    right_basis = right / jnp.sqrt(jnp.float32(token_total))
    row_count = weight.shape[0]
    offset = lax.axis_index("dp") * row_count
    basis_mine = lax.dynamic_slice_in_dim(left_basis, offset, row_count, 0)
    update = jnp.dot(basis_mine, right.T, precision=lax.Precision.HIGHEST)
    new_weight = weight.astype(jnp.float32) - learn_rate * update
    return (input_grad, right_basis, new_weight)


def solution(mesh):
    return jax.shard_map(
        body,
        mesh=mesh,
        in_specs=(P("dp", None), P("dp", "tensor"), P("dp", "tensor"), P("tensor", None)),
        out_specs=(P("dp", "tensor"), P("tensor", None), P("dp", "tensor")),
        check_vma=False,
    )
```

profile of v0, /device:TPU:0, one launch (start us, length us, event | category | flops | bytes accessed | tf_op | source)
XLA Modules:
  0.0 758.9 jit_solution(16477185492301689765)
XLA Ops:
  8.1 2.6 fusion.9
  10.6 0.1 copy-done.1
  10.8 0.7 fusion.3
  11.5 0.5 fusion.20
  11.9 1.5 fusion
  13.5 0.5 all-gather.2.cloned.1.call-update
  14.0 612.0 %all-reduce.3.cloned.1.call-done = f32[4096,64]{0,1:T(8,128)} async-done(((f32[4096,64]{0,1:T(8,128)}), f32[4096,64]{0,1:T(8,128)}) %all-reduce.3.cloned.1.call-update) | async-done | bytes 1048592 | tf_op jit(solution)/shard_map/psum | solution.py:42
  626.1 2.6 fusion.23
  628.7 0.1 copy.7
  628.8 5.8 cholesky.16
  634.7 0.6 compare_reduce_fusion
  635.3 0.7 fusion.12
  636.0 4.9 custom-call.7
  640.9 2.3 fusion.13
  643.2 0.8 fusion.6
  643.9 0.8 fusion.4
  644.7 0.7 copy-done.2
  645.4 0.4 fusion.17
  645.9 1.2 fusion.2
  647.2 15.3 %convolution_convert_fusion = bf16[256,4096]{1,0:T(8,128)(2,1)} fusion(bf16[256,3584]{1,0:T(8,128)(2,1)} %param.5, bf16[4096,3584]{1,0:T(8,128)(2,1)} %all-gather.2.cloned.1.call-done), kind=kOutput, calls=%fused_computation.1 | convolution fusion | flops 7517241344 | bytes 33292288 | tf_op jit(solution)/shard_map/dot_general | solution.py:29
  662.5 55.4 %all-reduce.5.cloned.1.call-done = bf16[3584,64]{0,1:T(8,128)(2,1)} async-done(((bf16[3584,64]{0,1:T(8,128)(2,1)}), bf16[3584,64]{0,1:T(8,128)(2,1)}) %all-reduce.5.cloned.1.call-update) | async-done | bytes 458768 | tf_op jit(solution)/shard_map/psum | solution.py:47
  717.9 7.5 multiply_subtract_fusion
  725.3 1.0 convert_multiply_fusion
  726.4 25.0 %reduce-scatter.2.cloned.1.call-done = bf16[256,1024]{1,0:T(8,128)(2,1)} async-done(((bf16[256,4096]{1,0:T(8,128)(2,1)}), bf16[256,1024]{1,0:T(8,128)(2,1)}) %reduce-scatter.2.cloned.1.call-update) | async-done | bytes 524304 | tf_op jit(solution)/shard_map/reduce_scatter | solution.py:35
  (18 shorter events, 0.3 us)
Async XLA Ops:
  8.0 3.4 copy-start
  8.0 2.6 copy-start.3
  8.0 618.1 %all-reduce.3.cloned.1.call-start = ((), (), s32[]{:S(2)}) async-start(), calls=%async_computation.3 | async-start | bytes 2097152 | tf_op jit(solution)/shard_map/psum | solution.py:42
  8.1 2.7 copy-start.1
  13.4 633.8 %all-gather.2.cloned.1.call-start = ((), (), s32[]{:S(2)}) async-start(), calls=%async_computation.1 | async-start | bytes 33030144 | tf_op jit(solution)/shard_map/all_gather | solution.py:31
  14.0 703.9 %all-reduce.5.cloned.1.call-start = ((), (), s32[]{:S(2)}) async-start(), calls=%async_computation.4 | async-start | bytes 917504 | tf_op jit(solution)/shard_map/psum | solution.py:47
  643.9 1.5 copy-start.2
  647.1 104.2 %reduce-scatter.2.cloned.1.call-start = ((), (), s32[]{:S(2)}) async-start(), calls=%async_computation.2 | async-start | bytes 2621440 | tf_op jit(solution)/shard_map/reduce_scatter | solution.py:35
  717.9 7.5 copy-start.4
Sparse Core Ops, SparseCore 0:
  14.6 611.4 all-reduce.2
Sparse Core Ops, SparseCore 1:
  15.4 564.2 all-gather.1
  647.2 70.6 all-reduce.4
  720.8 30.5 reduce-scatter.1
where the time goes:
time: 759 us
  waiting for transfers between devices  693 us (91%)
  matrix products  36 us (5%)
  between operations  15.8 us (2%)
  other arithmetic  13.1 us (2%)
    psum x1, waiting for transfers between devices, body(): left = lax.psum(left_part, ('dp', 'tensor'))  612 us
    psum x1, waiting for transfers between devices, body(): right = lax.psum(right_part.astype(jnp.bfloat16), 'dp').astype(jnp.float32)  55.4 us
    reduce_scatter x1, waiting for transfers between devices, body(): lax.psum_scatter(partial_input.astype(jnp.bfloat16), 'tensor', scatter_di...  25 us
    dot_general x1, matrix products, body(): lax.dot_general(grad_output, lax.all_gather(weight, 'dp', axis=0, tiled=T...  15.3 us
  transfers between devices with their start and end apart: 4, of which 3 were waited for; matrix products, arithmetic and copies ran while one was open for 6% of the time, Pallas kernels for 0%

commit v1 on v0

--- a/solution.py
+++ b/solution.py
@@ -26,15 +26,43 @@
 
 
 def body(activations, grad_output, weight, start_basis):
-    partial_input = lax.dot_general(
-        grad_output,
-        lax.all_gather(weight, "dp", axis=0, tiled=True),
-        (((1,), (1,)), ((), ())),
-        preferred_element_type=jnp.float32,
+    count = lax.axis_size("dp")
+    groups = count // 2
+    index = lax.axis_index("dp")
+    group = index // 2
+    swap = [(i, i + 1 - 2 * (i % 2)) for i in range(count)]
+    ahead = [(i, (i + 2) % count) for i in range(count)]
+    behind = [(i, (i - 2) % count) for i in range(count)]
+    other = lax.ppermute(weight, "dp", swap)
+    low = index % 2 == 0
+    weight_pair = jnp.concatenate(
+        [jnp.where(low, weight, other), jnp.where(low, other, weight)], axis=0
     )
-    input_grad = lax.psum_scatter(
-        partial_input.astype(jnp.bfloat16), "tensor", scatter_dimension=1, tiled=True
-    )
+    tokens = grad_output.shape[0]
+    half = tokens // 2
+    upper, under = grad_output[:half], grad_output[half:]
+    columns = weight_pair.shape[0]
+    partial = jnp.zeros((groups, tokens, columns), jnp.bfloat16)
+    for step in range(groups):
+        if step + 1 < groups:
+            next_upper = lax.ppermute(upper, "dp", ahead)
+            next_under = lax.ppermute(under, "dp", behind)
+        for piece, source, row in (
+            (upper, (group - step + groups) % groups, 0),
+            (under, (group + step) % groups, half),
+        ):
+            product = lax.dot_general(
+                piece, weight_pair, (((1,), (1,)), ((), ())), preferred_element_type=jnp.float32
+            ).astype(jnp.bfloat16)
+            partial = lax.dynamic_update_slice(partial, product[None], (source, row, 0))
+        if step + 1 < groups:
+            upper, under = next_upper, next_under
+    summed = lax.psum_scatter(partial, "tensor", scatter_dimension=1, tiled=True)
+    along = [[2 * g + b for g in range(groups)] for b in range(2)]
+    summed = lax.all_to_all(summed, "dp", 0, 0, axis_index_groups=along, tiled=True)
+    rows = summed.shape[1]
+    summed = summed.transpose(1, 0, 2).reshape(rows, groups * columns)
+    input_grad = lax.all_to_all(summed, "tensor", 1, 0, tiled=True)
     plain_dims = (((1,), (0,)), ((), ()))
     token_dims = (((0,), (0,)), ((), ()))
     thin_rows = thin_product(grad_output, start_basis, plain_dims)

time: 759 us -> 354 us (0.47)
  waiting for transfers between devices: 693 us -> 236 us
  starting transfers between devices: 0.17 us -> 21.6 us
  local copies, waits for them, and re-layouts: 0.96 us -> 14 us
  matrix products: 36 us -> 48.1 us
    psum x1, waiting for transfers between devices: 612 us -> 81.6 us  [body(): left = lax.psum(left_part, ('dp', 'tensor'))]
    ppermute x0 -> x7, waiting for transfers between devices: none -> 79.8 us  [the longest x3 40.5 us: body(): next_under = lax.ppermute(under, 'dp', behind)]
    reduce_scatter x1, waiting for transfers between devices: 25 us -> 0.03 us  [body(): lax.psum_scatter(partial, 'tensor', scatter_dimension=1, tiled=True)]
    psum x1, waiting for transfers between devices: 55.4 us -> 72.2 us  [body(): right = lax.psum(right_part.astype(jnp.bfloat16), 'dp').astype(jnp.float32)]
    dot_general x1 -> x8, matrix products: 15.3 us -> 29.8 us  [body(): lax.dot_general(piece, weight_pair, (((1,), (1,)), ((), ())), preferred_e...]
    ppermute x0 -> x7, starting transfers between devices: none -> 13 us  [the longest x3 5.06 us: body(): next_under = lax.ppermute(under, 'dp', behind)]
    all_to_all x0 -> x2, starting transfers between devices: none -> 8.31 us  [the longest x1 4.17 us: body(): lax.all_to_all(summed, 'dp', 0, 0, axis_index_groups=along, tiled=True)]
  transfers between devices with their start and end apart: 4 -> 12, of which waited for: 3 -> 8; matrix products, arithmetic and copies ran while one was open for 6% -> 22% of each run, Pallas kernels for 0% -> 0%
where the time goes in v1:
time: 354 us; the launch traced here: 353 us
  waiting for transfers between devices  236 us (67%)
  matrix products  48.1 us (14%)
  starting transfers between devices  21.6 us (6%)
  other arithmetic  17.8 us (5%)
  between operations  15.9 us (4%)
  local copies, waits for them, and re-layouts  14 us (4%)
    psum x1, waiting for transfers between devices, body(): left = lax.psum(left_part, ('dp', 'tensor'))  81.6 us
    psum x1, waiting for transfers between devices, body(): right = lax.psum(right_part.astype(jnp.bfloat16), 'dp').astype(jnp.float32)  72.2 us
    ppermute x3, waiting for transfers between devices, body(): next_under = lax.ppermute(under, 'dp', behind)  40.5 us
    ppermute x3, waiting for transfers between devices, body(): next_upper = lax.ppermute(upper, 'dp', ahead)  39.3 us
    dot_general x8, matrix products, body(): lax.dot_general(piece, weight_pair, (((1,), (1,)), ((), ())), preferred_e...  29.8 us
  transfers between devices with their start and end apart: 12, of which 8 were waited for; matrix products, arithmetic and copies ran while one was open for 22% of the time, Pallas kernels for 0%

profile of v1, /device:TPU:0, one launch (start us, length us, event | category | flops | bytes accessed | tf_op | source)
XLA Modules:
  0.0 353.0 jit_solution(11252358348205555578)
XLA Ops:
  8.1 3.0 collective-permute-start
  14.3 2.2 collective-permute-start.2
  17.2 20.7 %collective-permute-done.1 = bf16[128,3584]{1,0:T(8,128)(2,1)} collective-permute-done((bf16[128,3584]{1,0:T(8,128)(2,1)S(1)}, bf16[128,3584]{1,0:T(8,128)(2,1)}, u32[]{:S(2)}, u32[]{:S(2)}) %collective-permute-start.1) | collective-permute-done | bytes 917536 | tf_op jit(solution)/shard_map/ppermute | solution.py:48
  37.9 18.4 %collective-permute-done.2 = bf16[128,3584]{1,0:T(8,128)(2,1)} collective-permute-done((bf16[128,3584]{1,0:T(8,128)(2,1)S(1)}, bf16[128,3584]{1,0:T(8,128)(2,1)}, u32[]{:S(2)}, u32[]{:S(2)}) %collective-permute-start.2) | collective-permute-done | bytes 917536 | tf_op jit(solution)/shard_map/ppermute | solution.py:49
  56.4 2.8 collective-permute-start.4
  62.0 18.6 %collective-permute-done.3 = bf16[128,3584]{1,0:T(8,128)(2,1)} collective-permute-done((bf16[128,3584]{1,0:T(8,128)(2,1)}, bf16[128,3584]{1,0:T(8,128)(2,1)}, u32[]{:S(2)}, u32[]{:S(2)}) %collective-permute-start.3) | collective-permute-done | bytes 917536 | tf_op jit(solution)/shard_map/ppermute | solution.py:48
  80.6 3.3 collective-permute-start.5
  83.9 20.5 %collective-permute-done.4 = bf16[128,3584]{1,0:T(8,128)(2,1)} collective-permute-done((bf16[128,3584]{1,0:T(8,128)(2,1)}, bf16[128,3584]{1,0:T(8,128)(2,1)}, u32[]{:S(2)}, u32[]{:S(2)}) %collective-permute-start.4) | collective-permute-done | bytes 917536 | tf_op jit(solution)/shard_map/ppermute | solution.py:49
  104.5 3.7 %broadcast_select_fusion.1 = (bf16[512,3584]{1,0:T(8,128)(2,1)S(1)}, bf16[512,3584]{1,0:T(8,128)(2,1)S(1)}) fusion(bf16[512,3584]{1,0:T(8,128)(2,1)} %param.6, bf16[512,3584]{1,0:T(8,128)(2,1)} %collective-permute-done, pred[]{:T(512)S(6)} %eq.13), kind=kLoop, calls=%fused_computation.8 | loop fusion | flops 3670016 | bytes 14680065 | tf_op jit(solution)/shard_map/jit(_where)/select_n | solution.py:39
  113.5 5.4 %fusion.5 = bf16[1,128,1024]{1,2,0:T(8,128)(2,1)S(1)} fusion(bf16[128,3584]{1,0:T(8,128)(2,1)} %collective-permute-done.1, bf16[512,3584]{1,0:T(8,128)(2,1)} %copy-done.6, bf16[512,3584]{1,0:T(8,128)(2,1)} %copy-done.4), kind=kOutput, calls=%fused_computation.19 | convolution fusion | flops 954335232 | bytes 8519680 | tf_op jit(solution)/shard_map/dot_general | solution.py:54
  119.0 5.4 %fusion.6 = bf16[1,128,1024]{1,2,0:T(8,128)(2,1)S(1)} fusion(bf16[128,3584]{1,0:T(8,128)(2,1)} %collective-permute-done.2, bf16[512,3584]{1,0:T(8,128)(2,1)} %copy-done.6, bf16[512,3584]{1,0:T(8,128)(2,1)} %copy-done.4), kind=kOutput, calls=%fused_computation.20 | convolution fusion | flops 954335232 | bytes 8519680 | tf_op jit(solution)/shard_map/dot_general | solution.py:54
  128.4 4.5 %fusion.7 = bf16[1,128,1024]{1,2,0:T(8,128)(2,1)S(1)} fusion(bf16[128,3584]{1,0:T(8,128)(2,1)} %collective-permute-done.3, bf16[512,3584]{1,0:T(8,128)(2,1)} %copy-done.6, bf16[512,3584]{1,0:T(8,128)(2,1)S(1)} %copy-done.5), kind=kOutput, calls=%fused_computation.21 | convolution fusion | flops 954335232 | bytes 8519680 | tf_op jit(solution)/shard_map/dot_general | solution.py:54
  132.9 3.2 fusion.8
  136.2 3.2 fusion.9
  140.9 3.9 %fusion.10 = bf16[1,128,1024]{1,2,0:T(8,128)(2,1)} fusion(bf16[128,3584]{1,0:T(8,128)(2,1)} %collective-permute-done.6, bf16[512,3584]{1,0:T(8,128)(2,1)S(1)} %copy-done.7, bf16[512,3584]{1,0:T(8,128)(2,1)S(1)} %copy-done.5), kind=kOutput, calls=%fused_computation.24 | convolution fusion | flops 954335232 | bytes 8519680 | tf_op jit(solution)/shard_map/dot_general | solution.py:54
  150.3 81.6 %all-reduce.3.cloned.1.call-done = f32[4096,64]{0,1:T(8,128)} async-done(((f32[4096,64]{0,1:T(8,128)}), f32[4096,64]{0,1:T(8,128)}) %all-reduce.3.cloned.1.call-update) | async-done | bytes 1048592 | tf_op jit(solution)/shard_map/psum | solution.py:70
  232.0 2.5 fusion.34
  234.6 5.8 %cholesky.16 = f32[64,64]{1,0:T(8,128)S(1)} custom-call(f32[64,64]{1,0:T(8,128)S(1)} %fusion.23), custom_call_target="Cholesky" | custom-call | tf_op jit(solution)/shard_map/jit(cholesky)/cholesky | solution.py:11
  241.8 4.9 %custom-call.7 = f32[1,64,64]{1,2,0:T(8,128)S(1)} custom-call(f32[1,64,64]{2,1,0:T(8,128)S(1)} %fusion.20), custom_call_target="InvertDiagBlocksLowerTriangular" | custom-call | tf_op jit(solution)/shard_map/jit(_solve_triangular)/triangular_solve | solution.py:72
  246.7 2.3 fusion.21
  252.2 4.2 %all-to-all-start = ((bf16[4,64,1024]{2,1,0:T(8,128)(2,1)}), bf16[4,64,1024]{2,1,0:T(8,128)(2,1)}, u32[]{:S(2)}, u32[]{:S(2)}) async-start(bf16[4,64,1024]{2,1,0:T(8,128)(2,1)} %reduce-scatter.2.cloned.1.call-done), calls=%async_computation.1 | async-start | bytes 1048576 | tf_op jit(solution)/shard_map/all_to_all | solution.py:62
  256.4 72.2 %all-reduce.5.cloned.1.call-done = bf16[3584,64]{0,1:T(8,128)(2,1)} async-done(((bf16[3584,64]{0,1:T(8,128)(2,1)}), bf16[3584,64]{0,1:T(8,128)(2,1)}) %all-reduce.5.cloned.1.call-update) | async-done | bytes 458768 | tf_op jit(solution)/shard_map/psum | solution.py:75
  330.7 4.1 %all-to-all-start.1 = ((bf16[64,4,1024]{2,0,1:T(8,128)(2,1)}), bf16[64,4,1024]{2,0,1:T(8,128)(2,1)}, u32[]{:S(2)}, u32[]{:S(2)}) async-start(bf16[64,4,1024]{2,0,1:T(8,128)(2,1)} %bitcast.16), calls=%async_computation.2 | async-start | bytes 1048576 | tf_op jit(solution)/shard_map/all_to_all | solution.py:65
  334.8 7.0 %multiply_subtract_fusion = f32[512,3584]{1,0:T(8,128)} fusion(bf16[512,3584]{1,0:T(8,128)(2,1)} %param.6, bf16[3584,64]{0,1:T(8,128)(2,1)} %all-reduce.5.cloned.1.call-done, f32[4096,64]{0,1:T(8,128)S(1)} %fusion.21, s32[]{:T(128)S(6)} %select_n.90), kind=kOutput, calls=%fused_computation.1 | convolution fusion | flops 1414791168 | bytes 11599876 | tf_op jit(solution)/shard_map/dot_general | solution.py:81
  (68 shorter events, 33.4 us)
Async XLA Ops:
  8.0 51.9 %copy-start = (bf16[256,4096]{1,0:T(8,128)(2,1)S(1)}, bf16[256,4096]{1,0:T(8,128)(2,1)}, u32[]{:S(2)}) copy-start(bf16[256,4096]{1,0:T(8,128)(2,1)} %param.4) | copy-start | bytes 6291460
  8.0 8.5 %copy-start.8 = (f32[3584,64]{0,1:T(8,128)S(1)}, f32[3584,64]{0,1:T(8,128)}, u32[]{:S(2)}) copy-start(f32[3584,64]{0,1:T(8,128)} %param.7) | copy-start | bytes 2752516
  8.0 224.0 %all-reduce.3.cloned.1.call-start = ((), (), s32[]{:S(2)}) async-start(), calls=%async_computation.4 | async-start | bytes 2097152 | tf_op jit(solution)/shard_map/psum | solution.py:70
  8.1 8.5 %copy-start.1 = (bf16[256,3584]{1,0:T(8,128)(2,1)S(1)}, bf16[256,3584]{1,0:T(8,128)(2,1)}, u32[]{:S(2)}) copy-start(bf16[256,3584]{1,0:T(8,128)(2,1)} %param.5) | copy-start | bytes 5505028
  8.1 96.4 %collective-permute-start = (bf16[512,3584]{1,0:T(8,128)(2,1)}, bf16[512,3584]{1,0:T(8,128)(2,1)}, u32[]{:S(2)}, u32[]{:S(2)}) collective-permute-start(bf16[512,3584]{1,0:T(8,128)(2,1)} %param.6), channel_id=1, source_target_pairs={{0,4},{4,0},{8,12},{12,8},{16,20},{20,16},{24,28},{28,24},{1,5},{5... | collective-permute-start | bytes 11010056 | tf_op jit(solution)/shard_map/ppermute | solution.py:36
  12.7 25.3 %collective-permute-start.1 = (bf16[128,3584]{1,0:T(8,128)(2,1)S(1)}, bf16[128,3584]{1,0:T(8,128)(2,1)}, u32[]{:S(2)}, u32[]{:S(2)}) collective-permute-start(bf16[128,3584]{1,0:T(8,128)(2,1)S(1)} %get-tuple-element.6), channel_id=1, source_target_pairs={{0,8},{4,12},{8,16},{12,20},{16,24},{20,28},{24,0},{28,4},{1,9},{5... | collective-permute-start | bytes 2752520 | tf_op jit(solution)/shard_map/ppermute | solution.py:48
  14.3 42.1 %collective-permute-start.2 = (bf16[128,3584]{1,0:T(8,128)(2,1)S(1)}, bf16[128,3584]{1,0:T(8,128)(2,1)}, u32[]{:S(2)}, u32[]{:S(2)}) collective-permute-start(bf16[128,3584]{1,0:T(8,128)(2,1)S(1)} %get-tuple-element.5), channel_id=1, source_target_pairs={{0,24},{4,28},{8,0},{12,4},{16,8},{20,12},{24,16},{28,20},{1,25},{... | collective-permute-start | bytes 2752520 | tf_op jit(solution)/shard_map/ppermute | solution.py:49
  37.9 42.7 %collective-permute-start.3 = (bf16[128,3584]{1,0:T(8,128)(2,1)}, bf16[128,3584]{1,0:T(8,128)(2,1)}, u32[]{:S(2)}, u32[]{:S(2)}) collective-permute-start(bf16[128,3584]{1,0:T(8,128)(2,1)} %collective-permute-done.1), channel_id=1, source_target_pairs={{0,8},{4,12},{8,16},{12,20},{16,24},{20,28},{24,0},{28,4},{1,9},{5... | collective-permute-start | bytes 2752520 | tf_op jit(solution)/shard_map/ppermute | solution.py:48
  56.4 48.1 %collective-permute-start.4 = (bf16[128,3584]{1,0:T(8,128)(2,1)}, bf16[128,3584]{1,0:T(8,128)(2,1)}, u32[]{:S(2)}, u32[]{:S(2)}) collective-permute-start(bf16[128,3584]{1,0:T(8,128)(2,1)} %collective-permute-done.2), channel_id=1, source_target_pairs={{0,24},{4,28},{8,0},{12,4},{16,8},{20,12},{24,16},{28,20},{1,25},{... | collective-permute-start | bytes 2752520 | tf_op jit(solution)/shard_map/ppermute | solution.py:49
  61.8 190.4 %reduce-scatter.2.cloned.1.call-start = ((), (), s32[]{:S(2)}) async-start(), calls=%async_computation.3 | async-start | bytes 2621440 | tf_op jit(solution)/shard_map/reduce_scatter | solution.py:60
  62.0 46.1 %copy-start.2 = (bf16[256,3584]{1,0:T(8,128)(2,1)S(1)}, bf16[256,3584]{1,0:T(8,128)(2,1)}, u32[]{:S(2)}) copy-start(bf16[256,3584]{1,0:T(8,128)(2,1)} %param.5) | copy-start | bytes 5505028
  80.6 55.6 %collective-permute-start.5 = (bf16[128,3584]{1,0:T(8,128)(2,1)}, bf16[128,3584]{1,0:T(8,128)(2,1)}, u32[]{:S(2)}, u32[]{:S(2)}) collective-permute-start(bf16[128,3584]{1,0:T(8,128)(2,1)} %collective-permute-done.3), channel_id=1, source_target_pairs={{0,8},{4,12},{8,16},{12,20},{16,24},{20,28},{24,0},{28,4},{1,9},{5... | collective-permute-start | bytes 2752520 | tf_op jit(solution)/shard_map/ppermute | solution.py:48
  104.5 36.5 %collective-permute-start.6 = (bf16[128,3584]{1,0:T(8,128)(2,1)}, bf16[128,3584]{1,0:T(8,128)(2,1)}, u32[]{:S(2)}, u32[]{:S(2)}) collective-permute-start(bf16[128,3584]{1,0:T(8,128)(2,1)} %collective-permute-done.4), channel_id=1, source_target_pairs={{0,24},{4,28},{8,0},{12,4},{16,8},{20,12},{24,16},{28,20},{1,25},{... | collective-permute-start | bytes 2752520 | tf_op jit(solution)/shard_map/ppermute | solution.py:49
  108.1 2.1 copy-start.4
  108.1 3.0 copy-start.6
  124.6 3.8 %copy-start.5 = (bf16[512,3584]{1,0:T(8,128)(2,1)S(1)}, bf16[512,3584]{1,0:T(8,128)(2,1)}, u32[]{:S(2)}) copy-start(bf16[512,3584]{1,0:T(8,128)(2,1)} %copy-done.4) | copy-start | bytes 11010052
  128.4 4.5 %copy-start.7 = (bf16[512,3584]{1,0:T(8,128)(2,1)S(1)}, bf16[512,3584]{1,0:T(8,128)(2,1)}, u32[]{:S(2)}) copy-start(bf16[512,3584]{1,0:T(8,128)(2,1)} %copy-done.6) | copy-start | bytes 11010052
  150.1 178.5 %all-reduce.5.cloned.1.call-start = ((), (), s32[]{:S(2)}) async-start(), calls=%async_computation.5 | async-start | bytes 917504 | tf_op jit(solution)/shard_map/psum | solution.py:75
  249.0 1.5 copy-start.3
  252.2 78.4 %all-to-all-start = ((bf16[4,64,1024]{2,1,0:T(8,128)(2,1)}), bf16[4,64,1024]{2,1,0:T(8,128)(2,1)}, u32[]{:S(2)}, u32[]{:S(2)}) async-start(bf16[4,64,1024]{2,1,0:T(8,128)(2,1)} %reduce-scatter.2.cloned.1.call-done), calls=%async_computation.1 | async-start | bytes 1048576 | tf_op jit(solution)/shard_map/all_to_all | solution.py:62
  330.7 13.1 %all-to-all-start.1 = ((bf16[64,4,1024]{2,0,1:T(8,128)(2,1)}), bf16[64,4,1024]{2,0,1:T(8,128)(2,1)}, u32[]{:S(2)}, u32[]{:S(2)}) async-start(bf16[64,4,1024]{2,0,1:T(8,128)(2,1)} %bitcast.16), calls=%async_computation.2 | async-start | bytes 1048576 | tf_op jit(solution)/shard_map/all_to_all | solution.py:65
Sparse Core Ops, SparseCore 0:
  62.0 169.9 all-reduce.2
  252.3 76.2 all-reduce.4
Sparse Core Ops, SparseCore 1:
  150.2 29.8 reduce-scatter.1

commit v2 on v1

v2 whole, which is shorter than its diff:
```python
import jax
import jax.numpy as jnp
from jax import lax
from jax.sharding import PartitionSpec as P

learn_rate = 0.001
highest = lax.Precision.HIGHEST
tie = lax.optimization_barrier


def split_parts(values):
    upper_part = values.astype(jnp.bfloat16)
    lower_part = (values - upper_part.astype(jnp.float32)).astype(jnp.bfloat16)
    return (upper_part, lower_part)


def thin_product(thin_values, wide, wide_dim):
    rank = thin_values.shape[0]
    both = lax.dot_general(
        jnp.concatenate(split_parts(thin_values), axis=0),
        wide,
        (((1,), (wide_dim,)), ((), ())),
        preferred_element_type=jnp.float32,
    )
    return both[:rank] + both[rank:]


def spread(values, axis, groups=None):
    count = lax.axis_size(axis) if groups is None else len(groups[0])
    copies = jnp.broadcast_to(values[None], (count,) + values.shape)
    return lax.all_to_all(copies, axis, 0, 0, axis_index_groups=groups, tiled=True)


def body(activations, grad_output, weight, start_basis):
    count, width = lax.axis_size("dp"), lax.axis_size("tensor")
    index, lane = lax.axis_index("dp"), lax.axis_index("tensor")
    groups = count // 2
    group = index // 2
    tokens, depth = activations.shape
    row_count = weight.shape[0]
    half = tokens // 2
    swap = [(i, i + 1 - 2 * (i % 2)) for i in range(count)]
    ahead = [(i, (i + 2) % count) for i in range(count)]
    behind = [(i, (i - 2) % count) for i in range(count)]
    along = [[2 * g + b for g in range(groups)] for b in range(2)]
    share = depth // width
    activations_mine = lax.dynamic_slice_in_dim(activations, lane * share, share, 1)

    def left_stage():
        thin_rows = spread(thin_product(start_basis.T, grad_output, 1), "tensor").sum(0)
        left_part = thin_product(thin_rows, activations_mine, 0)
        rank = left_part.shape[0]
        pieces = left_part.reshape(rank, count, share // count).transpose(1, 0, 2)
        left_piece = lax.all_to_all(pieces, "dp", 0, 0, tiled=True).sum(0)
        return spread(left_piece, "dp").transpose(1, 0, 2).reshape(rank, share)

    def basis_stage(left):
        rank = left.shape[0]
        raw_proj = thin_product(left, activations_mine, 1)
        gram_part = lax.dot_general(left, left, (((1,), (1,)), ((), ())), precision=highest)
        both = spread(jnp.concatenate([raw_proj, gram_part], axis=1), "tensor").sum(0)
        lower = jnp.linalg.cholesky(both[:, tokens:])
        inverse = jax.scipy.linalg.solve_triangular(lower, jnp.eye(rank, dtype=jnp.float32), lower=True)
        token_proj = jnp.dot(inverse, both[:, :tokens], precision=highest)
        per_share = share // row_count
        rows = lax.dynamic_slice_in_dim(left, (index % per_share) * row_count, row_count, 1)
        rows = lax.dynamic_index_in_dim(spread(rows, "tensor"), index // per_share, 0, False)
        basis_mine = jnp.dot(inverse, rows, precision=highest)
        return spread(token_proj, "dp", along), basis_mine

    other = lax.ppermute(weight, "dp", swap)
    low = index % 2 == 0
    weight_pair = jnp.concatenate(
        [jnp.where(low, weight, other), jnp.where(low, other, weight)], axis=0
    )
    columns = weight_pair.shape[0]
    upper, under = grad_output[:half], grad_output[half:]
    gathered = jnp.zeros((groups, 2, half, grad_output.shape[1]), jnp.bfloat16)
    summed = jnp.zeros((groups, 2, half // width, columns), jnp.bfloat16)
    for step in range(groups):
        if step + 1 < groups:
            next_upper = lax.ppermute(upper, "dp", ahead)
            next_under = lax.ppermute(under, "dp", behind)
        sources = ((group - step + groups) % groups, (group + step) % groups)
        products = []
        for place, (piece, source) in enumerate(zip((upper, under), sources)):
            gathered = lax.dynamic_update_slice(gathered, piece[None, None], (source, place, 0, 0))
            product = lax.dot_general(
                piece, weight_pair, (((1,), (1,)), ((), ())), preferred_element_type=jnp.float32
            )
            products.append(product.astype(jnp.bfloat16).reshape(width, half // width, columns))
        parts = lax.all_to_all(jnp.stack(products, axis=1), "tensor", 0, 0, tiled=True)
        total = parts.astype(jnp.float32).sum(0).astype(jnp.bfloat16)
        for place, source in enumerate(sources):
            summed = lax.dynamic_update_slice(summed, total[place][None, None], (source, place, 0, 0))
        if step == 0:
            left = left_stage()
            next_upper, next_under, left = tie((next_upper, next_under, left))
        if step == 1:
            token_proj, basis_mine = basis_stage(left)
            next_upper, next_under, token_proj = tie((next_upper, next_under, token_proj))
        if step + 1 < groups:
            upper, under = next_upper, next_under

    rank = start_basis.shape[1]
    right_part = thin_product(
        token_proj.transpose(1, 0, 2).reshape(rank, groups * tokens),
        gathered.reshape(groups * tokens, -1),
        0,
    ).astype(jnp.bfloat16)
    right_other = lax.ppermute(right_part, "dp", swap)
    right = right_part.astype(jnp.float32) + right_other.astype(jnp.float32)
    right_basis = (right / jnp.sqrt(jnp.float32(tokens * count))).T

    moved = lax.all_to_all(summed, "dp", 0, 0, axis_index_groups=along, tiled=True)
    moved = moved.reshape(groups, 2 * (half // width), columns).transpose(1, 0, 2)
    moved = moved.reshape(2, half // width, width, share).transpose(2, 0, 1, 3)
    moved = lax.all_to_all(moved, "tensor", 0, 0, tiled=True)
    input_grad = moved.transpose(1, 0, 2, 3).reshape(tokens, share)

    basis_upper, basis_lower = split_parts(basis_mine)
    update = lax.dot_general(
        jnp.concatenate([basis_upper, basis_upper, basis_lower, basis_lower], axis=0),
        jnp.concatenate([right_part, right_other, right_part, right_other], axis=0),
        (((0,), (0,)), ((), ())),
        preferred_element_type=jnp.float32,
    )
    new_weight = weight.astype(jnp.float32) - learn_rate * update
    return (input_grad, right_basis, new_weight)


def solution(mesh):
    return jax.shard_map(
        body,
        mesh=mesh,
        in_specs=(P("dp", None), P("dp", "tensor"), P("dp", "tensor"), P("tensor", None)),
        out_specs=(P("dp", "tensor"), P("tensor", None), P("dp", "tensor")),
        check_vma=False,
    )
```

time: 354 us -> 331 us (0.935)
  waiting for transfers between devices: 236 us -> 165 us
  starting transfers between devices: 21.6 us -> 61.7 us
  local copies, waits for them, and re-layouts: 14 us -> 32.7 us
  between operations: 15.9 us -> 1.11 us
  other arithmetic: 17.8 us -> 24.1 us
    psum x2 -> x0, waiting for transfers between devices: 154 us -> none  [the longest x1 81.6 us: body(): left = lax.psum(left_part, ('dp', 'tensor'))]
    all_to_all x1 -> x11, waiting for transfers between devices: 1.87 us -> 120 us  [the longest x1 72.2 us: left_stage(): left_piece = lax.all_to_all(pieces, 'dp', 0, 0, tiled=True).sum(0)]
    all_to_all x1 -> x11, starting transfers between devices: 4.15 us -> 42.8 us  [the longest x5 20.3 us: spread(): lax.all_to_all(copies, axis, 0, 0, axis_index_groups=groups, tiled=True)]
    ppermute x3, waiting for transfers between devices: 40.5 us -> 15.6 us  [body(): next_under = lax.ppermute(under, 'dp', behind)]
    ppermute x3, waiting for transfers between devices: 39.3 us -> 17.1 us  [body(): next_upper = lax.ppermute(upper, 'dp', ahead)]
    dynamic_update_slice x8 -> x16, local copies, waits for them, and re-layouts: 5.82 us -> 18.9 us  [the longest x8 13.8 us: body(): lax.dynamic_update_slice(gathered, piece[None, None], (source, place, 0, 0))]
    all_to_all x1, waiting for transfers between devices: 0.01 us -> 12 us  [body(): lax.all_to_all(summed, 'dp', 0, 0, axis_index_groups=along, tiled=True)]
    ppermute x3, starting transfers between devices: 5.06 us -> 10.4 us  [body(): next_under = lax.ppermute(under, 'dp', behind)]
  transfers between devices with their start and end apart: 12 -> 20, of which waited for: 8 -> 11; matrix products, arithmetic and copies ran while one was open for 22% -> 29% of each run, Pallas kernels for 0% -> 0%
where the time goes in v2:
time: 331 us; the launch traced here: 330 us
  waiting for transfers between devices  165 us (50%)
  starting transfers between devices  61.7 us (19%)
  matrix products  45.2 us (14%)
  local copies, waits for them, and re-layouts  32.7 us (10%)
  other arithmetic  24.1 us (7%)
    all_to_all x1, waiting for transfers between devices, left_stage(): left_piece = lax.all_to_all(pieces, 'dp', 0, 0, tiled=True).sum(0)  72.2 us
    dot_general x8, matrix products, body(): lax.dot_general(piece, weight_pair, (((1,), (1,)), ((), ())), preferred_e...  29.5 us
    all_to_all x5, waiting for transfers between devices, spread(): lax.all_to_all(copies, axis, 0, 0, axis_index_groups=groups, tiled=True)  24.8 us
    all_to_all x4, waiting for transfers between devices, body(): lax.all_to_all(jnp.stack(products, axis=1), 'tensor', 0, 0, tiled=True)  21.5 us
    all_to_all x5, starting transfers between devices, spread(): lax.all_to_all(copies, axis, 0, 0, axis_index_groups=groups, tiled=True)  20.3 us
    ppermute x3, waiting for transfers between devices, body(): next_upper = lax.ppermute(upper, 'dp', ahead)  17.1 us
    ppermute x3, waiting for transfers between devices, body(): next_under = lax.ppermute(under, 'dp', behind)  15.6 us
    all_to_all x4, starting transfers between devices, body(): lax.all_to_all(jnp.stack(products, axis=1), 'tensor', 0, 0, tiled=True)  13.9 us
  transfers between devices with their start and end apart: 20, of which 11 were waited for; matrix products, arithmetic and copies ran while one was open for 29% of the time, Pallas kernels for 0%

profile of v2, /device:TPU:0, one launch (start us, length us, event | category | flops | bytes accessed | tf_op | source)
XLA Modules:
  0.0 329.9 jit_solution(12063492064925574302)
XLA Ops:
  5.0 4.2 %all-to-all-start.1 = ((f32[4,64,256]{2,1,0:T(8,128)}), f32[4,64,256]{2,1,0:T(8,128)S(1)}, u32[]{:S(2)}, u32[]{:S(2)}) async-start(f32[4,64,256]{2,1,0:T(8,128)} %broadcast_in_dim.63), calls=%async_computation.1 | async-start | bytes 524288 | tf_op jit(solution)/shard_map/all_to_all | solution.py:31
  11.7 4.2 %collective-permute-start.2 = (bf16[128,3584]{1,0:T(8,128)(2,1)}, bf16[128,3584]{1,0:T(8,128)(2,1)}, u32[]{:S(2)}, u32[]{:S(2)}) collective-permute-start(bf16[128,3584]{1,0:T(8,128)(2,1)} %get-tuple-element.27), channel_id=1, source_target_pairs={{0,24},{4,28},{8,0},{12,4},{16,8},{20,12},{24,16},{28,20},{1,25},{... | collective-permute-start | bytes 2752520 | tf_op jit(solution)/shard_map/ppermute | solution.py:83
  18.5 5.1 %all-to-all-start.2 = ((f32[8,64,128]{2,1,0:T(8,128)}), f32[8,64,128]{2,1,0:T(8,128)S(1)}, u32[]{:S(2)}, u32[]{:S(2)}) async-start(f32[8,64,128]{2,1,0:T(8,128)} %bitcast_bitcast_fusion), calls=%async_computation.2 | async-start | bytes 524288 | tf_op jit(solution)/shard_map/all_to_all | solution.py:54
  23.6 3.7 %broadcast_in_dim.67 = bf16[4,2,128,3584]{3,2,1,0:T(8,128)(2,1)} broadcast(bf16[]{:T(256)} %constant.131.clone.1), dimensions={} | broadcast | bytes 7340034 | tf_op jit(solution)/shard_map/broadcast_in_dim | solution.py:78
  28.3 72.2 %all-to-all-done.2 = f32[8,64,128]{2,1,0:T(8,128)S(1)} async-done(((f32[8,64,128]{2,1,0:T(8,128)}), f32[8,64,128]{2,1,0:T(8,128)S(1)}, u32[]{:S(2)}, u32[]{:S(2)}) %all-to-all-start.2) | async-done | bytes 262176 | tf_op jit(solution)/shard_map/all_to_all | solution.py:54
  101.2 5.7 %all-to-all-start.3 = ((f32[8,64,128]{2,1,0:T(8,128)}), f32[8,64,128]{2,1,0:T(8,128)S(1)}, u32[]{:S(2)}, u32[]{:S(2)}) async-start(f32[8,64,128]{2,1,0:T(8,128)} %broadcast_in_dim.64), calls=%async_computation.3 | async-start | bytes 524288 | tf_op jit(solution)/shard_map/all_to_all | solution.py:31
  109.1 6.2 %all-to-all-done.3 = f32[8,64,128]{2,1,0:T(8,128)S(1)} async-done(((f32[8,64,128]{2,1,0:T(8,128)}), f32[8,64,128]{2,1,0:T(8,128)S(1)}, u32[]{:S(2)}, u32[]{:S(2)}) %all-to-all-start.3) | async-done | bytes 262176 | tf_op jit(solution)/shard_map/all_to_all | solution.py:31
  132.2 5.8 %cholesky.17 = f32[64,64]{1,0:T(8,128)S(1)} custom-call(f32[64,64]{1,0:T(8,128)S(1)} %fusion.51), custom_call_target="Cholesky" | custom-call | tf_op jit(solution)/shard_map/jit(cholesky)/cholesky | solution.py:62
  139.4 4.9 %custom-call.7 = f32[1,64,64]{1,2,0:T(8,128)S(1)} custom-call(f32[1,64,64]{2,1,0:T(8,128)S(1)} %fusion.48), custom_call_target="InvertDiagBlocksLowerTriangular" | custom-call | tf_op jit(solution)/shard_map/jit(_solve_triangular)/triangular_solve | solution.py:63
  152.0 17.2 %all-to-all-done.6 = f32[4,64,256]{2,1,0:T(8,128)S(1)} async-done(((f32[4,64,256]{2,1,0:T(8,128)}), f32[4,64,256]{2,1,0:T(8,128)S(1)}, u32[]{:S(2)}, u32[]{:S(2)}) %all-to-all-start.6) | async-done | bytes 262176 | tf_op jit(solution)/shard_map/all_to_all | solution.py:31
  177.4 17.1 %collective-permute-done.5 = bf16[128,3584]{1,0:T(8,128)(2,1)S(1)} collective-permute-done((bf16[128,3584]{1,0:T(8,128)(2,1)}, bf16[128,3584]{1,0:T(8,128)(2,1)S(1)}, u32[]{:S(2)}, u32[]{:S(2)}) %collective-permute-start.5) | collective-permute-done | bytes 917536 | tf_op jit(solution)/shard_map/ppermute | solution.py:82
  195.5 15.6 %collective-permute-done.6 = bf16[128,3584]{1,0:T(8,128)(2,1)S(1)} collective-permute-done((bf16[128,3584]{1,0:T(8,128)(2,1)}, bf16[128,3584]{1,0:T(8,128)(2,1)S(1)}, u32[]{:S(2)}, u32[]{:S(2)}) %collective-permute-start.6) | collective-permute-done | bytes 917536 | tf_op jit(solution)/shard_map/ppermute | solution.py:83
  212.3 4.4 %fusion.21 = f32[128,3584]{1,0:T(8,128)S(1)} fusion(bf16[1024,3584]{1,0:T(8,128)(2,1)} %bitcast.47, bf16[64,1024]{1,0:T(8,128)(2,1)S(1)} %get-tuple-element.17, bf16[64,1024]{1,0:T(8,128)(2,1)S(1)} %get-tuple-element.18), kind=kOutput, calls=%fused_computation.52 | convolution fusion | flops 940048384 | bytes 9437184 | tf_op jit(solution)/shard_map/dot_general | solution.py:19
  225.1 4.3 %convolution_convert_fusion.5 = bf16[128,1024]{1,0:T(8,128)(2,1)} fusion(bf16[128,3584]{1,0:T(8,128)(2,1)} %collective-permute-done.1, bf16[512,3584]{1,0:T(8,128)(2,1)S(1)} %get-tuple-element.26, bf16[512,3584]{1,0:T(8,128)(2,1)S(1)} %get-tuple-element.25), kind=kOutput, calls=%fused_computation.16 | convolution fusion | flops 954335232 | bytes 8519680 | tf_op jit(solution)/shard_map/dot_general | solution.py:88
  229.4 4.3 %convolution_convert_fusion.4 = bf16[128,1024]{1,0:T(8,128)(2,1)} fusion(bf16[128,3584]{1,0:T(8,128)(2,1)} %collective-permute-done.2, bf16[512,3584]{1,0:T(8,128)(2,1)S(1)} %get-tuple-element.26, bf16[512,3584]{1,0:T(8,128)(2,1)S(1)} %get-tuple-element.25), kind=kOutput, calls=%fused_computation.15 | convolution fusion | flops 954335232 | bytes 8519680 | tf_op jit(solution)/shard_map/dot_general | solution.py:88
  233.7 4.3 %convolution_convert_fusion.3 = bf16[128,1024]{1,0:T(8,128)(2,1)} fusion(bf16[128,3584]{1,0:T(8,128)(2,1)} %collective-permute-done.3, bf16[512,3584]{1,0:T(8,128)(2,1)S(1)} %get-tuple-element.26, bf16[512,3584]{1,0:T(8,128)(2,1)S(1)} %get-tuple-element.25), kind=kOutput, calls=%fused_computation.14 | convolution fusion | flops 954335232 | bytes 8519680 | tf_op jit(solution)/shard_map/dot_general | solution.py:88
  238.1 4.3 %convolution_convert_fusion.2 = bf16[128,1024]{1,0:T(8,128)(2,1)} fusion(bf16[128,3584]{1,0:T(8,128)(2,1)} %collective-permute-done.4, bf16[512,3584]{1,0:T(8,128)(2,1)S(1)} %get-tuple-element.26, bf16[512,3584]{1,0:T(8,128)(2,1)S(1)} %get-tuple-element.25), kind=kOutput, calls=%fused_computation.13 | convolution fusion | flops 954335232 | bytes 8519680 | tf_op jit(solution)/shard_map/dot_general | solution.py:88
  249.2 4.9 %convolution_convert_fusion.1 = bf16[128,1024]{1,0:T(8,128)(2,1)S(1)} fusion(bf16[128,3584]{1,0:T(8,128)(2,1)S(1)} %collective-permute-done.5, bf16[512,3584]{1,0:T(8,128)(2,1)} %copy-done.7, bf16[512,3584]{1,0:T(8,128)(2,1)} %copy-done.5), kind=kOutput, calls=%fused_computation.12 | convolution fusion | flops 954335232 | bytes 8519680 | tf_op jit(solution)/shard_map/dot_general | solution.py:88
  265.4 6.6 %all-to-all-done.4 = bf16[4,2,32,1024]{3,2,1,0:T(8,128)(2,1)S(1)} async-done(((bf16[4,2,32,1024]{3,2,1,0:T(8,128)(2,1)}), bf16[4,2,32,1024]{3,2,1,0:T(8,128)(2,1)S(1)}, u32[]{:S(2)}, u32[]{:S(2)}) %all-to-all-start.4) | async-done | bytes 524320 | tf_op jit(solution)/shard_map/all_to_all | solution.py:92
  276.9 7.4 %all-to-all-done.7 = bf16[4,2,32,1024]{3,2,1,0:T(8,128)(2,1)S(1)} async-done(((bf16[4,2,32,1024]{3,2,1,0:T(8,128)(2,1)}), bf16[4,2,32,1024]{3,2,1,0:T(8,128)(2,1)S(1)}, u32[]{:S(2)}, u32[]{:S(2)}) %all-to-all-start.7) | async-done | bytes 524320 | tf_op jit(solution)/shard_map/all_to_all | solution.py:92
  289.1 7.4 %all-to-all-done.8 = bf16[4,2,32,1024]{3,2,1,0:T(8,128)(2,1)S(1)} async-done(((bf16[4,2,32,1024]{3,2,1,0:T(8,128)(2,1)}), bf16[4,2,32,1024]{3,2,1,0:T(8,128)(2,1)S(1)}, u32[]{:S(2)}, u32[]{:S(2)}) %all-to-all-start.8) | async-done | bytes 524320 | tf_op jit(solution)/shard_map/all_to_all | solution.py:92
  298.0 4.1 %all-to-all-start.9 = ((bf16[4,2,32,1024]{3,2,1,0:T(8,128)(2,1)}), bf16[4,2,32,1024]{3,2,1,0:T(8,128)(2,1)}, u32[]{:S(2)}, u32[]{:S(2)}) async-start(bf16[4,2,32,1024]{3,2,1,0:T(8,128)(2,1)} %fusion.35), calls=%async_computation.9 | async-start | bytes 1048576 | tf_op jit(solution)/shard_map/all_to_all | solution.py:115
  304.8 12.0 %all-to-all-done.9 = bf16[4,2,32,1024]{3,2,1,0:T(8,128)(2,1)} async-done(((bf16[4,2,32,1024]{3,2,1,0:T(8,128)(2,1)}), bf16[4,2,32,1024]{3,2,1,0:T(8,128)(2,1)}, u32[]{:S(2)}, u32[]{:S(2)}) %all-to-all-start.9) | async-done | bytes 524320 | tf_op jit(solution)/shard_map/all_to_all | solution.py:115
  320.2 6.8 %multiply_subtract_fusion = f32[512,3584]{1,0:T(8,128)} fusion(bf16[512,3584]{1,0:T(8,128)(2,1)} %param.6, bf16[64,3584]{1,0:T(8,128)(2,1)} %collective-permute-done.7, bf16[64,3584]{1,0:T(8,128)(2,1)} %fusion.7, bf16[64,512]{1,0:T(8,128)(2,1)S(1)} %copy-done.15, bf16[64,512]{1,0:T(8,128)(2,1)S(1)} %copy-done.16), kind=kOutput, calls=%fused_computation.1 | convolution fusion | flops 953417728 | bytes 12058624 | tf_op jit(solution)/shard_map/dot_general | solution.py:122
  (125 shorter events, 95.8 us)
Async XLA Ops:
  5.0 12.5 %all-to-all-start.1 = ((f32[4,64,256]{2,1,0:T(8,128)}), f32[4,64,256]{2,1,0:T(8,128)S(1)}, u32[]{:S(2)}, u32[]{:S(2)}) async-start(f32[4,64,256]{2,1,0:T(8,128)} %broadcast_in_dim.63), calls=%async_computation.1 | async-start | bytes 524288 | tf_op jit(solution)/shard_map/all_to_all | solution.py:31
  11.7 103.6 %collective-permute-start.2 = (bf16[128,3584]{1,0:T(8,128)(2,1)}, bf16[128,3584]{1,0:T(8,128)(2,1)}, u32[]{:S(2)}, u32[]{:S(2)}) collective-permute-start(bf16[128,3584]{1,0:T(8,128)(2,1)} %get-tuple-element.27), channel_id=1, source_target_pairs={{0,24},{4,28},{8,0},{12,4},{16,8},{20,12},{24,16},{28,20},{1,25},{... | collective-permute-start | bytes 2752520 | tf_op jit(solution)/shard_map/ppermute | solution.py:83
  16.0 99.3 %collective-permute-start.1 = (bf16[128,3584]{1,0:T(8,128)(2,1)S(1)}, bf16[128,3584]{1,0:T(8,128)(2,1)}, u32[]{:S(2)}, u32[]{:S(2)}) collective-permute-start(bf16[128,3584]{1,0:T(8,128)(2,1)S(1)} %get-tuple-element.28), channel_id=1, source_target_pairs={{0,8},{4,12},{8,16},{12,20},{16,24},{20,28},{24,0},{28,4},{1,9},{5... | collective-permute-start | bytes 2752520 | tf_op jit(solution)/shard_map/ppermute | solution.py:82
  16.0 204.1 %collective-permute-start = (bf16[512,3584]{1,0:T(8,128)(2,1)}, bf16[512,3584]{1,0:T(8,128)(2,1)}, u32[]{:S(2)}, u32[]{:S(2)}) collective-permute-start(bf16[512,3584]{1,0:T(8,128)(2,1)} %param.6), channel_id=1, source_target_pairs={{0,4},{4,0},{8,12},{12,8},{16,20},{20,16},{24,28},{28,24},{1,5},{5... | collective-permute-start | bytes 11010056 | tf_op jit(solution)/shard_map/ppermute | solution.py:71
  18.5 81.9 %all-to-all-start.2 = ((f32[8,64,128]{2,1,0:T(8,128)}), f32[8,64,128]{2,1,0:T(8,128)S(1)}, u32[]{:S(2)}, u32[]{:S(2)}) async-start(f32[8,64,128]{2,1,0:T(8,128)} %bitcast_bitcast_fusion), calls=%async_computation.2 | async-start | bytes 524288 | tf_op jit(solution)/shard_map/all_to_all | solution.py:54
  101.2 14.1 %all-to-all-start.3 = ((f32[8,64,128]{2,1,0:T(8,128)}), f32[8,64,128]{2,1,0:T(8,128)S(1)}, u32[]{:S(2)}, u32[]{:S(2)}) async-start(f32[8,64,128]{2,1,0:T(8,128)} %broadcast_in_dim.64), calls=%async_computation.3 | async-start | bytes 524288 | tf_op jit(solution)/shard_map/all_to_all | solution.py:31
  116.9 10.9 %all-to-all-start.5 = ((f32[4,64,320]{2,1,0:T(8,128)}), f32[4,64,320]{2,1,0:T(8,128)S(1)}, u32[]{:S(2)}, u32[]{:S(2)}) async-start(f32[4,64,320]{2,1,0:T(8,128)} %broadcast_in_dim.65), calls=%async_computation.5 | async-start | bytes 786432 | tf_op jit(solution)/shard_map/all_to_all | solution.py:31
  120.3 48.9 %collective-permute-start.3 = (bf16[128,3584]{1,0:T(8,128)(2,1)}, bf16[128,3584]{1,0:T(8,128)(2,1)}, u32[]{:S(2)}, u32[]{:S(2)}) collective-permute-start(bf16[128,3584]{1,0:T(8,128)(2,1)} %collective-permute-done.1), channel_id=1, source_target_pairs={{0,8},{4,12},{8,16},{12,20},{16,24},{20,28},{24,0},{28,4},{1,9},{5... | collective-permute-start | bytes 2752520 | tf_op jit(solution)/shard_map/ppermute | solution.py:82
  121.3 47.9 %collective-permute-start.4 = (bf16[128,3584]{1,0:T(8,128)(2,1)}, bf16[128,3584]{1,0:T(8,128)(2,1)}, u32[]{:S(2)}, u32[]{:S(2)}) collective-permute-start(bf16[128,3584]{1,0:T(8,128)(2,1)} %collective-permute-done.2), channel_id=1, source_target_pairs={{0,24},{4,28},{8,0},{12,4},{16,8},{20,12},{24,16},{28,20},{1,25},{... | collective-permute-start | bytes 2752520 | tf_op jit(solution)/shard_map/ppermute | solution.py:83
  128.6 16.1 %all-to-all-start.11 = ((f32[4,64,512]{2,1,0:T(8,128)}), f32[4,64,512]{2,1,0:T(8,128)S(1)}, u32[]{:S(2)}, u32[]{:S(2)}) async-start(f32[4,64,512]{2,1,0:T(8,128)} %broadcast_in_dim.76), calls=%async_computation.11 | async-start | bytes 1048576 | tf_op jit(solution)/shard_map/all_to_all | solution.py:31
  145.5 23.7 %all-to-all-start.6 = ((f32[4,64,256]{2,1,0:T(8,128)}), f32[4,64,256]{2,1,0:T(8,128)S(1)}, u32[]{:S(2)}, u32[]{:S(2)}) async-start(f32[4,64,256]{2,1,0:T(8,128)} %broadcast_in_dim.66), calls=%async_computation.6 | async-start | bytes 524288 | tf_op jit(solution)/shard_map/all_to_all | solution.py:31
  169.2 25.3 %collective-permute-start.5 = (bf16[128,3584]{1,0:T(8,128)(2,1)}, bf16[128,3584]{1,0:T(8,128)(2,1)S(1)}, u32[]{:S(2)}, u32[]{:S(2)}) collective-permute-start(bf16[128,3584]{1,0:T(8,128)(2,1)} %collective-permute-done.3), channel_id=1, source_target_pairs={{0,8},{4,12},{8,16},{12,20},{16,24},{20,28},{24,0},{28,4},{1,9},{5... | collective-permute-start | bytes 2752520 | tf_op jit(solution)/shard_map/ppermute | solution.py:82
  169.7 41.4 %collective-permute-start.6 = (bf16[128,3584]{1,0:T(8,128)(2,1)}, bf16[128,3584]{1,0:T(8,128)(2,1)S(1)}, u32[]{:S(2)}, u32[]{:S(2)}) collective-permute-start(bf16[128,3584]{1,0:T(8,128)(2,1)} %collective-permute-done.4), channel_id=1, source_target_pairs={{0,24},{4,28},{8,0},{12,4},{16,8},{20,12},{24,16},{28,20},{1,25},{... | collective-permute-start | bytes 2752520 | tf_op jit(solution)/shard_map/ppermute | solution.py:83
  218.8 83.3 %collective-permute-start.7 = (bf16[64,3584]{1,0:T(8,128)(2,1)}, bf16[64,3584]{1,0:T(8,128)(2,1)}, u32[]{:S(2)}, u32[]{:S(2)}) collective-permute-start(bf16[64,3584]{1,0:T(8,128)(2,1)} %fusion.7), channel_id=1, source_target_pairs={{0,4},{4,0},{8,12},{12,8},{16,20},{20,16},{24,28},{28,24},{1,5},{5... | collective-permute-start | bytes 1376264 | tf_op jit(solution)/shard_map/ppermute | solution.py:111
  222.6 19.8 %copy-start.5 = (bf16[512,3584]{1,0:T(8,128)(2,1)}, bf16[512,3584]{1,0:T(8,128)(2,1)S(1)}, u32[]{:S(2)}) copy-start(bf16[512,3584]{1,0:T(8,128)(2,1)S(1)} %get-tuple-element.25) | copy-start | bytes 11010052
  222.6 19.8 %copy-start.7 = (bf16[512,3584]{1,0:T(8,128)(2,1)}, bf16[512,3584]{1,0:T(8,128)(2,1)S(1)}, u32[]{:S(2)}) copy-start(bf16[512,3584]{1,0:T(8,128)(2,1)S(1)} %get-tuple-element.26) | copy-start | bytes 11010052
  245.7 14.0 %all-to-all-start = ((bf16[4,2,32,1024]{3,2,1,0:T(8,128)(2,1)}), bf16[4,2,32,1024]{3,2,1,0:T(8,128)(2,1)S(1)}, u32[]{:S(2)}, u32[]{:S(2)}) async-start(bf16[4,2,32,1024]{3,2,1,0:T(8,128)(2,1)} %pad_maximum_fusion.1), calls=%async_computation | async-start | bytes 1048576 | tf_op jit(solution)/shard_map/all_to_all | solution.py:92
  258.0 62.2 %copy-start.15 = (bf16[64,512]{1,0:T(8,128)(2,1)S(1)}, bf16[64,512]{1,0:T(8,128)(2,1)}, u32[]{:S(2)}) copy-start(bf16[64,512]{1,0:T(8,128)(2,1)} %get-tuple-element.15) | copy-start | bytes 196612
  258.0 62.2 %copy-start.16 = (bf16[64,512]{1,0:T(8,128)(2,1)S(1)}, bf16[64,512]{1,0:T(8,128)(2,1)}, u32[]{:S(2)}) copy-start(bf16[64,512]{1,0:T(8,128)(2,1)} %get-tuple-element.16) | copy-start | bytes 196612
  259.7 12.3 %all-to-all-start.4 = ((bf16[4,2,32,1024]{3,2,1,0:T(8,128)(2,1)}), bf16[4,2,32,1024]{3,2,1,0:T(8,128)(2,1)S(1)}, u32[]{:S(2)}, u32[]{:S(2)}) async-start(bf16[4,2,32,1024]{3,2,1,0:T(8,128)(2,1)} %pad_maximum_fusion.2), calls=%async_computation.4 | async-start | bytes 1048576 | tf_op jit(solution)/shard_map/all_to_all | solution.py:92
  272.0 12.3 %all-to-all-start.7 = ((bf16[4,2,32,1024]{3,2,1,0:T(8,128)(2,1)}), bf16[4,2,32,1024]{3,2,1,0:T(8,128)(2,1)S(1)}, u32[]{:S(2)}, u32[]{:S(2)}) async-start(bf16[4,2,32,1024]{3,2,1,0:T(8,128)(2,1)} %pad_maximum_fusion.3), calls=%async_computation.7 | async-start | bytes 1048576 | tf_op jit(solution)/shard_map/all_to_all | solution.py:92
  284.3 12.3 %all-to-all-start.8 = ((bf16[4,2,32,1024]{3,2,1,0:T(8,128)(2,1)}), bf16[4,2,32,1024]{3,2,1,0:T(8,128)(2,1)S(1)}, u32[]{:S(2)}, u32[]{:S(2)}) async-start(bf16[4,2,32,1024]{3,2,1,0:T(8,128)(2,1)} %pad_maximum_fusion.4), calls=%async_computation.8 | async-start | bytes 1048576 | tf_op jit(solution)/shard_map/all_to_all | solution.py:92
  298.0 18.8 %all-to-all-start.9 = ((bf16[4,2,32,1024]{3,2,1,0:T(8,128)(2,1)}), bf16[4,2,32,1024]{3,2,1,0:T(8,128)(2,1)}, u32[]{:S(2)}, u32[]{:S(2)}) async-start(bf16[4,2,32,1024]{3,2,1,0:T(8,128)(2,1)} %fusion.35), calls=%async_computation.9 | async-start | bytes 1048576 | tf_op jit(solution)/shard_map/all_to_all | solution.py:115
  316.7 12.3 %all-to-all-start.10 = ((bf16[4,2,32,1024]{3,2,1,0:T(8,128)(2,1)}), bf16[4,2,32,1024]{3,2,1,0:T(8,128)(2,1)S(1)}, u32[]{:S(2)}, u32[]{:S(2)}) async-start(bf16[4,2,32,1024]{3,2,1,0:T(8,128)(2,1)} %all-to-all-done.9), calls=%async_computation.10 | async-start | bytes 1048576 | tf_op jit(solution)/shard_map/all_to_all | solution.py:118
  (13 other events, 62.0 us)

commit v3 on v2

--- a/solution.py
+++ b/solution.py
@@ -66,41 +66,62 @@
         rows = lax.dynamic_slice_in_dim(left, (index % per_share) * row_count, row_count, 1)
         rows = lax.dynamic_index_in_dim(spread(rows, "tensor"), index // per_share, 0, False)
         basis_mine = jnp.dot(inverse, rows, precision=highest)
-        return spread(token_proj, "dp", along), basis_mine
+        return token_proj, basis_mine
 
-    other = lax.ppermute(weight, "dp", swap)
+    left = left_stage()
+    weight_sent, grad_sent, left = tie((weight, grad_output, left))
+    other = lax.ppermute(weight_sent, "dp", swap)
     low = index % 2 == 0
     weight_pair = jnp.concatenate(
         [jnp.where(low, weight, other), jnp.where(low, other, weight)], axis=0
     )
     columns = weight_pair.shape[0]
-    upper, under = grad_output[:half], grad_output[half:]
+    piece_rows = half // width
+    upper, under = grad_sent[:half], grad_sent[half:]
     gathered = jnp.zeros((groups, 2, half, grad_output.shape[1]), jnp.bfloat16)
-    summed = jnp.zeros((groups, 2, half // width, columns), jnp.bfloat16)
+    returned = jnp.zeros((groups, 2, piece_rows, columns), jnp.bfloat16)
+
+    def reduced(pieces):
+        product = lax.dot_general(
+            jnp.concatenate(pieces, axis=0), weight_pair, (((1,), (1,)), ((), ())),
+            preferred_element_type=jnp.float32,
+        ).astype(jnp.bfloat16)
+        product = product.reshape(len(pieces), width, piece_rows, columns).transpose(1, 0, 2, 3)
+        parts = lax.all_to_all(product, "tensor", 0, 0, tiled=True)
+        return parts.astype(jnp.float32).sum(0).astype(jnp.bfloat16)
+
+    def give_back(returned, total, step):
+        for place, sign in enumerate((1, -1)):
+            value = total[place]
+            if step:
+                back = [(i, (i - 2 * sign * step) % count) for i in range(count)]
+                value = lax.ppermute(value, "dp", back)
+            source = (group + sign * step + groups) % groups
+            returned = lax.dynamic_update_slice(returned, value[None, None], (source, place, 0, 0))
+        return returned
+
+    pieces = []
     for step in range(groups):
-        if step + 1 < groups:
-            next_upper = lax.ppermute(upper, "dp", ahead)
-            next_under = lax.ppermute(under, "dp", behind)
+        if step == groups - 1:
+            total = reduced(pieces)
+            for earlier in range(step):
+                returned = give_back(returned, total[2 * earlier : 2 * earlier + 2], earlier)
+            total = reduced([upper, under])
+            returned = give_back(returned, total, step)
         sources = ((group - step + groups) % groups, (group + step) % groups)
-        products = []
         for place, (piece, source) in enumerate(zip((upper, under), sources)):
             gathered = lax.dynamic_update_slice(gathered, piece[None, None], (source, place, 0, 0))
-            product = lax.dot_general(
-                piece, weight_pair, (((1,), (1,)), ((), ())), preferred_element_type=jnp.float32
-            )
-            products.append(product.astype(jnp.bfloat16).reshape(width, half // width, columns))
-        parts = lax.all_to_all(jnp.stack(products, axis=1), "tensor", 0, 0, tiled=True)
-        total = parts.astype(jnp.float32).sum(0).astype(jnp.bfloat16)
-        for place, source in enumerate(sources):
-            summed = lax.dynamic_update_slice(summed, total[place][None, None], (source, place, 0, 0))
+            pieces.append(piece)
+        if step + 1 < groups:
+            if step == 1:
+                upper, under, token_proj = tie((upper, under, token_proj))
+            if step == groups - 2:
+                upper, under, weight_pair = tie((upper, under, weight_pair))
+            upper = lax.ppermute(upper, "dp", ahead)
+            under = lax.ppermute(under, "dp", behind)
         if step == 0:
-            left = left_stage()
-            next_upper, next_under, left = tie((next_upper, next_under, left))
-        if step == 1:
             token_proj, basis_mine = basis_stage(left)
-            next_upper, next_under, token_proj = tie((next_upper, next_under, token_proj))
-        if step + 1 < groups:
-            upper, under = next_upper, next_under
+    token_proj = spread(token_proj, "dp", along)
 
     rank = start_basis.shape[1]
     right_part = thin_product(
@@ -112,7 +133,7 @@
     right = right_part.astype(jnp.float32) + right_other.astype(jnp.float32)
     right_basis = (right / jnp.sqrt(jnp.float32(tokens * count))).T
 
-    moved = lax.all_to_all(summed, "dp", 0, 0, axis_index_groups=along, tiled=True)
+    moved = returned
     moved = moved.reshape(groups, 2 * (half // width), columns).transpose(1, 0, 2)
     moved = moved.reshape(2, half // width, width, share).transpose(2, 0, 1, 3)
     moved = lax.all_to_all(moved, "tensor", 0, 0, tiled=True)

time: 331 us -> 254 us (0.77)
  waiting for transfers between devices: 165 us -> 84.3 us
  blocking collectives: 0 us -> 14.9 us
  matrix products: 45.2 us -> 30.6 us
  starting transfers between devices: 61.7 us -> 52 us
  local copies, waits for them, and re-layouts: 32.7 us -> 39.5 us
  other arithmetic: 24.1 us -> 30.5 us
    all_to_all x6 -> x2, waiting for transfers between devices: 106 us -> 0.01 us  [reduced(): parts = lax.all_to_all(product, 'tensor', 0, 0, tiled=True)]
    all_to_all x5, waiting for transfers between devices: 24.8 us -> 48.2 us  [spread(): lax.all_to_all(copies, axis, 0, 0, axis_index_groups=groups, tiled=True)]
    all_to_all x6 -> x2, starting transfers between devices: 23.1 us -> 8 us  [reduced(): parts = lax.all_to_all(product, 'tensor', 0, 0, tiled=True)]
    all_to_all x0 -> x1, blocking collectives: none -> 14.9 us  [left_stage(): left_piece = lax.all_to_all(pieces, 'dp', 0, 0, tiled=True).sum(0)]
    dot_general x8 -> x2, matrix products: 29.5 us -> 15.2 us  [reduced(): lax.dot_general(jnp.concatenate(pieces, axis=0), weight_pair, (((1,), (1,...]
    concatenate x0 -> x1, other arithmetic: none -> 6.68 us  [body(): jnp.concatenate([jnp.where(low, weight, other), jnp.where(low, other, wei...]
    ppermute x7 -> x13, starting transfers between devices: 13.4 us -> 20 us  [the longest x6 8.68 us: give_back(): value = lax.ppermute(value, 'dp', back)]
    unnamed x35 -> x13, local copies, waits for them, and re-layouts: 2.11 us -> 7.17 us
  transfers between devices with their start and end apart: 20 -> 22, of which waited for: 11 -> 10; matrix products, arithmetic and copies ran while one was open for 29% -> 30% of each run, Pallas kernels for 0% -> 0%
where the time goes in v3:
time: 254 us; the launch traced here: 253 us
  waiting for transfers between devices  84.3 us (33%)
  starting transfers between devices  52 us (20%)
  local copies, waits for them, and re-layouts  39.5 us (16%)
  matrix products  30.6 us (12%)
  other arithmetic  30.5 us (12%)
  blocking collectives  14.9 us (6%)
    all_to_all x5, waiting for transfers between devices, spread(): lax.all_to_all(copies, axis, 0, 0, axis_index_groups=groups, tiled=True)  48.2 us
    ppermute x3, waiting for transfers between devices, body(): under = lax.ppermute(under, 'dp', behind)  28.1 us
    all_to_all x5, starting transfers between devices, spread(): lax.all_to_all(copies, axis, 0, 0, axis_index_groups=groups, tiled=True)  18.8 us
    dot_general x2, matrix products, reduced(): lax.dot_general(jnp.concatenate(pieces, axis=0), weight_pair, (((1,), (1,...  15.2 us
    all_to_all x1, blocking collectives, left_stage(): left_piece = lax.all_to_all(pieces, 'dp', 0, 0, tiled=True).sum(0)  14.9 us
    dynamic_update_slice x8, local copies, waits for them, and re-layouts, body(): lax.dynamic_update_slice(gathered, piece[None, None], (source, place, 0, 0))  11.6 us
    ppermute x6, starting transfers between devices, give_back(): value = lax.ppermute(value, 'dp', back)  8.68 us
    all_to_all x2, starting transfers between devices, reduced(): parts = lax.all_to_all(product, 'tensor', 0, 0, tiled=True)  8 us
  transfers between devices with their start and end apart: 22, of which 10 were waited for; matrix products, arithmetic and copies ran while one was open for 30% of the time, Pallas kernels for 0%

profile of v3, /device:TPU:0, one launch (start us, length us, event | category | flops | bytes accessed | tf_op | source)
XLA Modules:
  0.0 252.8 jit_solution(4427925534331525659)
XLA Ops:
  5.0 4.2 %all-to-all-start = ((f32[4,64,256]{2,1,0:T(8,128)}), f32[4,64,256]{2,1,0:T(8,128)S(1)}, u32[]{:S(2)}, u32[]{:S(2)}) async-start(f32[4,64,256]{2,1,0:T(8,128)} %broadcast_in_dim.81), calls=%async_computation | async-start | bytes 524288 | tf_op jit(solution)/shard_map/all_to_all | solution.py:31
  9.2 6.0 %all-to-all-done = f32[4,64,256]{2,1,0:T(8,128)S(1)} async-done(((f32[4,64,256]{2,1,0:T(8,128)}), f32[4,64,256]{2,1,0:T(8,128)S(1)}, u32[]{:S(2)}, u32[]{:S(2)}) %all-to-all-start) | async-done | bytes 262176 | tf_op jit(solution)/shard_map/all_to_all | solution.py:31
  15.6 14.9 %all_to_all.45 = f32[8,64,128]{2,1,0:T(8,128)S(1)} all-to-all(f32[8,64,128]{2,1,0:T(8,128)S(1)} %bitcast_bitcast_fusion), channel_id=1, replica_groups=mesh['dp'=8,'tensor'=4] {'dp'}, dimensions={0} | all-to-all | bytes 524288 | tf_op jit(solution)/shard_map/all_to_all | solution.py:54
  31.3 3.6 %all-to-all-start.2 = ((f32[8,64,128]{2,1,0:T(8,128)}), f32[8,64,128]{2,1,0:T(8,128)S(1)}, u32[]{:S(2)}, u32[]{:S(2)}) async-start(f32[8,64,128]{2,1,0:T(8,128)} %broadcast_in_dim.82), calls=%async_computation.2 | async-start | bytes 524288 | tf_op jit(solution)/shard_map/all_to_all | solution.py:31
  34.9 8.5 %all-to-all-done.2 = f32[8,64,128]{2,1,0:T(8,128)S(1)} async-done(((f32[8,64,128]{2,1,0:T(8,128)}), f32[8,64,128]{2,1,0:T(8,128)S(1)}, u32[]{:S(2)}, u32[]{:S(2)}) %all-to-all-start.2) | async-done | bytes 262176 | tf_op jit(solution)/shard_map/all_to_all | solution.py:31
  54.6 4.1 %all-to-all-start.3 = ((f32[4,64,320]{2,1,0:T(8,128)}), f32[4,64,320]{2,1,0:T(8,128)}, u32[]{:S(2)}, u32[]{:S(2)}) async-start(f32[4,64,320]{2,1,0:T(8,128)} %broadcast_in_dim.83), calls=%async_computation.3 | async-start | bytes 786432 | tf_op jit(solution)/shard_map/all_to_all | solution.py:31
  60.3 3.6 %broadcast_in_dim.91 = bf16[4,2,128,3584]{3,2,1,0:T(8,128)(2,1)} broadcast(bf16[]{:T(256)} %constant.160.clone.1), dimensions={} | broadcast | bytes 7340034 | tf_op jit(solution)/shard_map/broadcast_in_dim | solution.py:81
  68.0 3.5 %all-to-all-start.8 = ((f32[4,64,512]{2,1,0:T(8,128)}), f32[4,64,512]{2,1,0:T(8,128)S(1)}, u32[]{:S(2)}, u32[]{:S(2)}) async-start(f32[4,64,512]{2,1,0:T(8,128)} %broadcast_in_dim.100), calls=%async_computation.8 | async-start | bytes 1048576 | tf_op jit(solution)/shard_map/all_to_all | solution.py:31
  72.6 5.8 %cholesky.17 = f32[64,64]{1,0:T(8,128)S(1)} custom-call(f32[64,64]{1,0:T(8,128)S(1)} %fusion.52), custom_call_target="Cholesky" | custom-call | tf_op jit(solution)/shard_map/jit(cholesky)/cholesky | solution.py:62
  79.7 4.9 %custom-call.7 = f32[1,64,64]{1,2,0:T(8,128)S(1)} custom-call(f32[1,64,64]{2,1,0:T(8,128)S(1)} %fusion.49), custom_call_target="InvertDiagBlocksLowerTriangular" | custom-call | tf_op jit(solution)/shard_map/jit(_solve_triangular)/triangular_solve | solution.py:63
  85.9 3.8 %collective-permute-done.1 = bf16[128,3584]{1,0:T(8,128)(2,1)S(1)} collective-permute-done((bf16[128,3584]{1,0:T(8,128)(2,1)}, bf16[128,3584]{1,0:T(8,128)(2,1)S(1)}, u32[]{:S(2)}, u32[]{:S(2)}) %collective-permute-start.1) | collective-permute-done | bytes 917536 | tf_op jit(solution)/shard_map/ppermute | solution.py:121
  94.3 3.4 %all-to-all-start.7 = ((f32[4,64,256]{2,1,0:T(8,128)}), f32[4,64,256]{2,1,0:T(8,128)S(1)}, u32[]{:S(2)}, u32[]{:S(2)}) async-start(f32[4,64,256]{2,1,0:T(8,128)} %broadcast_in_dim.90), calls=%async_computation.7 | async-start | bytes 524288 | tf_op jit(solution)/shard_map/all_to_all | solution.py:31
  104.0 33.6 %all-to-all-done.7 = f32[4,64,256]{2,1,0:T(8,128)S(1)} async-done(((f32[4,64,256]{2,1,0:T(8,128)}), f32[4,64,256]{2,1,0:T(8,128)S(1)}, u32[]{:S(2)}, u32[]{:S(2)}) %all-to-all-start.7) | async-done | bytes 262176 | tf_op jit(solution)/shard_map/all_to_all | solution.py:31
  141.7 5.5 %broadcast_select_fusion.1 = (bf16[512,3584]{1,0:T(8,128)(2,1)}, bf16[512,3584]{1,0:T(8,128)(2,1)}) fusion(bf16[512,3584]{1,0:T(8,128)(2,1)S(1)} %copy-done.3, bf16[512,3584]{1,0:T(8,128)(2,1)} %collective-permute-done.4, pred[]{:T(512)S(6)} %eq.23), kind=kLoop, calls=%fused_computation.3 | loop fusion | flops 3670016 | bytes 14680065 | tf_op jit(solution)/shard_map/jit(_where)/select_n | solution.py:76
  147.2 6.7 %pad_maximum_fusion = bf16[1024,3584]{1,0:T(8,128)(2,1)} fusion(bf16[512,3584]{1,0:T(8,128)(2,1)} %get-tuple-element.32, bf16[512,3584]{1,0:T(8,128)(2,1)} %get-tuple-element.31), kind=kLoop, calls=%fused_computation | loop fusion | flops 14680064 | bytes 14680064 | tf_op jit(solution)/shard_map/concatenate | solution.py:75
  155.9 9.8 %convolution_convert_fusion = bf16[768,1024]{1,0:T(8,128)(2,1)S(1)} fusion(bf16[768,3584]{1,0:T(8,128)(2,1)} %constant_dynamic-update-slice_fusion, bf16[1024,3584]{1,0:T(8,128)(2,1)} %pad_maximum_fusion), kind=kOutput, calls=%fused_computation.15 | convolution fusion | flops 5637931008 | bytes 14417920 | tf_op jit(solution)/shard_map/dot_general | solution.py:85
  166.9 4.5 %all-to-all-start.4 = ((bf16[4,6,32,1024]{3,2,1,0:T(8,128)(2,1)}), bf16[4,6,32,1024]{3,2,1,0:T(8,128)(2,1)}, u32[]{:S(2)}, u32[]{:S(2)}) async-start(bf16[4,6,32,1024]{3,2,1,0:T(8,128)(2,1)} %bitcast.111), calls=%async_computation.4 | async-start | bytes 3145728 | tf_op jit(solution)/shard_map/all_to_all | solution.py:90
  171.5 24.3 %collective-permute-done.10 = bf16[128,3584]{1,0:T(8,128)(2,1)S(1)} collective-permute-done((bf16[128,3584]{1,0:T(8,128)(2,1)S(1)}, bf16[128,3584]{1,0:T(8,128)(2,1)S(1)}, u32[]{:S(2)}, u32[]{:S(2)}) %collective-permute-start.10) | collective-permute-done | bytes 917536 | tf_op jit(solution)/shard_map/ppermute | solution.py:121
  195.8 5.5 %fusion.11 = bf16[256,1024]{1,0:T(8,128)(2,1)S(1)} fusion(bf16[1024,3584]{1,0:T(8,128)(2,1)} %pad_maximum_fusion, bf16[128,3584]{1,0:T(8,128)(2,1)S(1)} %collective-permute-done.10, bf16[128,3584]{1,0:T(8,128)(2,1)} %collective-permute-done.9), kind=kOutput, calls=%fused_computation.17 | convolution fusion | flops 1882980352 | bytes 9699328 | tf_op jit(solution)/shard_map/dot_general | solution.py:85
  205.3 4.2 %fusion.28 = f32[128,3584]{1,0:T(8,128)S(1)} fusion(bf16[1024,3584]{1,0:T(8,128)(2,1)} %bitcast.39, bf16[64,1024]{1,0:T(8,128)(2,1)S(1)} %get-tuple-element.23, bf16[64,1024]{1,0:T(8,128)(2,1)S(1)} %get-tuple-element.24), kind=kOutput, calls=%fused_computation.48 | convolution fusion | flops 940048384 | bytes 9437184 | tf_op jit(solution)/shard_map/dot_general | solution.py:19
  212.1 3.5 %all-to-all-start.5 = ((bf16[4,2,32,1024]{3,2,1,0:T(8,128)(2,1)}), bf16[4,2,32,1024]{3,2,1,0:T(8,128)(2,1)S(1)}, u32[]{:S(2)}, u32[]{:S(2)}) async-start(bf16[4,2,32,1024]{3,2,1,0:T(8,128)(2,1)} %bitcast.112), calls=%async_computation.5 | async-start | bytes 1048576 | tf_op jit(solution)/shard_map/all_to_all | solution.py:90
  233.1 3.7 %collective-permute-start.12 = (bf16[32,1024]{1,0:T(8,128)(2,1)S(1)}, bf16[32,1024]{1,0:T(8,128)(2,1)S(1)}, u32[]{:S(2)}, u32[]{:S(2)}) collective-permute-start(bf16[32,1024]{1,0:T(8,128)(2,1)S(1)} %get-tuple-element.39), channel_id=1, source_target_pairs={{0,24},{4,28},{8,0},{12,4},{16,8},{20,12},{24,16},{28,20},{1,25},{... | collective-permute-start | bytes 196616 | tf_op jit(solution)/shard_map/ppermute | solution.py:98
  239.7 3.5 %all-to-all-start.6 = ((bf16[4,2,32,1024]{3,2,1,0:T(8,128)(2,1)}), bf16[4,2,32,1024]{3,2,1,0:T(8,128)(2,1)S(1)}, u32[]{:S(2)}, u32[]{:S(2)}) async-start(bf16[4,2,32,1024]{3,2,1,0:T(8,128)(2,1)} %bitcast_dynamic-update-slice_fusion.8), calls=%async_computation.6 | async-start | bytes 1048576 | tf_op jit(solution)/shard_map/all_to_all | solution.py:139
  244.2 6.7 %multiply_subtract_fusion = f32[512,3584]{1,0:T(8,128)} fusion(bf16[512,3584]{1,0:T(8,128)(2,1)} %param.6, bf16[64,3584]{1,0:T(8,128)(2,1)S(1)} %collective-permute-done.13, bf16[64,3584]{1,0:T(8,128)(2,1)} %fusion.14, bf16[64,512]{1,0:T(8,128)(2,1)S(1)} %get-tuple-element.21, bf16[64,512]{1,0:T(8,128)(2,1)} %get-tuple-element.22), kind=kOutput, calls=%fused_computation.1 | convolution fusion | flops 953417728 | bytes 12058624 | tf_op jit(solution)/shard_map/dot_general | solution.py:143
  (102 shorter events, 74.0 us)
Async XLA Ops:
  0.6 14.7 %copy-start = (bf16[256,4096]{1,0:T(8,128)(2,1)S(1)}, bf16[256,4096]{1,0:T(8,128)(2,1)}, u32[]{:S(2)}) copy-start(bf16[256,4096]{1,0:T(8,128)(2,1)} %param.4) | copy-start | bytes 6291460
  5.0 10.3 %all-to-all-start = ((f32[4,64,256]{2,1,0:T(8,128)}), f32[4,64,256]{2,1,0:T(8,128)S(1)}, u32[]{:S(2)}, u32[]{:S(2)}) async-start(f32[4,64,256]{2,1,0:T(8,128)} %broadcast_in_dim.81), calls=%async_computation | async-start | bytes 524288 | tf_op jit(solution)/shard_map/all_to_all | solution.py:31
  31.3 12.2 %all-to-all-start.2 = ((f32[8,64,128]{2,1,0:T(8,128)}), f32[8,64,128]{2,1,0:T(8,128)S(1)}, u32[]{:S(2)}, u32[]{:S(2)}) async-start(f32[8,64,128]{2,1,0:T(8,128)} %broadcast_in_dim.82), calls=%async_computation.2 | async-start | bytes 524288 | tf_op jit(solution)/shard_map/all_to_all | solution.py:31
  49.6 36.4 %collective-permute-start = (bf16[128,3584]{1,0:T(8,128)(2,1)}, bf16[128,3584]{1,0:T(8,128)(2,1)}, u32[]{:S(2)}, u32[]{:S(2)}) collective-permute-start(bf16[128,3584]{1,0:T(8,128)(2,1)} %get-tuple-element.34), channel_id=1, source_target_pairs={{0,8},{4,12},{8,16},{12,20},{16,24},{20,28},{24,0},{28,4},{1,9},{5... | collective-permute-start | bytes 2752520 | tf_op jit(solution)/shard_map/ppermute | solution.py:120
  50.7 39.0 %collective-permute-start.1 = (bf16[128,3584]{1,0:T(8,128)(2,1)}, bf16[128,3584]{1,0:T(8,128)(2,1)S(1)}, u32[]{:S(2)}, u32[]{:S(2)}) collective-permute-start(bf16[128,3584]{1,0:T(8,128)(2,1)} %get-tuple-element.33), channel_id=1, source_target_pairs={{0,24},{4,28},{8,0},{12,4},{16,8},{20,12},{24,16},{28,20},{1,25},{... | collective-permute-start | bytes 2752520 | tf_op jit(solution)/shard_map/ppermute | solution.py:121
  53.8 12.3 %copy-start.2 = (bf16[256,3584]{1,0:T(8,128)(2,1)S(1)}, bf16[256,3584]{1,0:T(8,128)(2,1)}, u32[]{:S(2)}) copy-start(bf16[256,3584]{1,0:T(8,128)(2,1)} %param.5) | copy-start | bytes 5505028
  54.6 12.5 %all-to-all-start.3 = ((f32[4,64,320]{2,1,0:T(8,128)}), f32[4,64,320]{2,1,0:T(8,128)}, u32[]{:S(2)}, u32[]{:S(2)}) async-start(f32[4,64,320]{2,1,0:T(8,128)} %broadcast_in_dim.83), calls=%async_computation.3 | async-start | bytes 786432 | tf_op jit(solution)/shard_map/all_to_all | solution.py:31
  58.7 83.0 %collective-permute-start.4 = (bf16[512,3584]{1,0:T(8,128)(2,1)}, bf16[512,3584]{1,0:T(8,128)(2,1)}, u32[]{:S(2)}, u32[]{:S(2)}) collective-permute-start(bf16[512,3584]{1,0:T(8,128)(2,1)} %param.6), channel_id=1, source_target_pairs={{0,4},{4,0},{8,12},{12,8},{16,20},{20,16},{24,28},{28,24},{1,5},{5... | collective-permute-start | bytes 11010056 | tf_op jit(solution)/shard_map/ppermute | solution.py:73
  68.0 17.1 %all-to-all-start.8 = ((f32[4,64,512]{2,1,0:T(8,128)}), f32[4,64,512]{2,1,0:T(8,128)S(1)}, u32[]{:S(2)}, u32[]{:S(2)}) async-start(f32[4,64,512]{2,1,0:T(8,128)} %broadcast_in_dim.100), calls=%async_computation.8 | async-start | bytes 1048576 | tf_op jit(solution)/shard_map/all_to_all | solution.py:31
  89.7 47.9 %collective-permute-start.2 = (bf16[128,3584]{1,0:T(8,128)(2,1)}, bf16[128,3584]{1,0:T(8,128)(2,1)S(1)}, u32[]{:S(2)}, u32[]{:S(2)}) collective-permute-start(bf16[128,3584]{1,0:T(8,128)(2,1)} %collective-permute-done), channel_id=1, source_target_pairs={{0,8},{4,12},{8,16},{12,20},{16,24},{20,28},{24,0},{28,4},{1,9},{5... | collective-permute-start | bytes 2752520 | tf_op jit(solution)/shard_map/ppermute | solution.py:120
  91.4 47.2 %collective-permute-start.3 = (bf16[128,3584]{1,0:T(8,128)(2,1)S(1)}, bf16[128,3584]{1,0:T(8,128)(2,1)S(1)}, u32[]{:S(2)}, u32[]{:S(2)}) collective-permute-start(bf16[128,3584]{1,0:T(8,128)(2,1)S(1)} %collective-permute-done.1), channel_id=1, source_target_pairs={{0,24},{4,28},{8,0},{12,4},{16,8},{20,12},{24,16},{28,20},{1,25},{... | collective-permute-start | bytes 2752520 | tf_op jit(solution)/shard_map/ppermute | solution.py:121
  94.3 43.3 %all-to-all-start.7 = ((f32[4,64,256]{2,1,0:T(8,128)}), f32[4,64,256]{2,1,0:T(8,128)S(1)}, u32[]{:S(2)}, u32[]{:S(2)}) async-start(f32[4,64,256]{2,1,0:T(8,128)} %broadcast_in_dim.90), calls=%async_computation.7 | async-start | bytes 524288 | tf_op jit(solution)/shard_map/all_to_all | solution.py:31
  153.8 41.9 %collective-permute-start.10 = (bf16[128,3584]{1,0:T(8,128)(2,1)S(1)}, bf16[128,3584]{1,0:T(8,128)(2,1)S(1)}, u32[]{:S(2)}, u32[]{:S(2)}) collective-permute-start(bf16[128,3584]{1,0:T(8,128)(2,1)S(1)} %collective-permute-done.3), channel_id=1, source_target_pairs={{0,24},{4,28},{8,0},{12,4},{16,8},{20,12},{24,16},{28,20},{1,25},{... | collective-permute-start | bytes 2752520 | tf_op jit(solution)/shard_map/ppermute | solution.py:121
  155.6 40.2 %collective-permute-start.9 = (bf16[128,3584]{1,0:T(8,128)(2,1)S(1)}, bf16[128,3584]{1,0:T(8,128)(2,1)}, u32[]{:S(2)}, u32[]{:S(2)}) collective-permute-start(bf16[128,3584]{1,0:T(8,128)(2,1)S(1)} %collective-permute-done.2), channel_id=1, source_target_pairs={{0,8},{4,12},{8,16},{12,20},{16,24},{20,28},{24,0},{28,4},{1,9},{5... | collective-permute-start | bytes 2752520 | tf_op jit(solution)/shard_map/ppermute | solution.py:120
  166.9 45.1 %all-to-all-start.4 = ((bf16[4,6,32,1024]{3,2,1,0:T(8,128)(2,1)}), bf16[4,6,32,1024]{3,2,1,0:T(8,128)(2,1)}, u32[]{:S(2)}, u32[]{:S(2)}) async-start(bf16[4,6,32,1024]{3,2,1,0:T(8,128)(2,1)} %bitcast.111), calls=%async_computation.4 | async-start | bytes 3145728 | tf_op jit(solution)/shard_map/all_to_all | solution.py:90
  210.3 32.8 %collective-permute-start.13 = (bf16[64,3584]{1,0:T(8,128)(2,1)}, bf16[64,3584]{1,0:T(8,128)(2,1)S(1)}, u32[]{:S(2)}, u32[]{:S(2)}) collective-permute-start(bf16[64,3584]{1,0:T(8,128)(2,1)} %fusion.14), channel_id=1, source_target_pairs={{0,4},{4,0},{8,12},{12,8},{16,20},{20,16},{24,28},{28,24},{1,5},{5... | collective-permute-start | bytes 1376264 | tf_op jit(solution)/shard_map/ppermute | solution.py:132
  212.1 20.1 %all-to-all-start.5 = ((bf16[4,2,32,1024]{3,2,1,0:T(8,128)(2,1)}), bf16[4,2,32,1024]{3,2,1,0:T(8,128)(2,1)S(1)}, u32[]{:S(2)}, u32[]{:S(2)}) async-start(bf16[4,2,32,1024]{3,2,1,0:T(8,128)(2,1)} %bitcast.112), calls=%async_computation.5 | async-start | bytes 1048576 | tf_op jit(solution)/shard_map/all_to_all | solution.py:90
  219.4 5.6 %collective-permute-start.5 = (bf16[32,1024]{1,0:T(8,128)(2,1)S(1)}, bf16[32,1024]{1,0:T(8,128)(2,1)S(1)}, u32[]{:S(2)}, u32[]{:S(2)}) collective-permute-start(bf16[32,1024]{1,0:T(8,128)(2,1)S(1)} %get-tuple-element.38), channel_id=1, source_target_pairs={{0,24},{4,28},{8,0},{12,4},{16,8},{20,12},{24,16},{28,20},{1,25},{... | collective-permute-start | bytes 196616 | tf_op jit(solution)/shard_map/ppermute | solution.py:98
  221.3 6.8 %collective-permute-start.6 = (bf16[32,1024]{1,0:T(8,128)(2,1)S(1)}, bf16[32,1024]{1,0:T(8,128)(2,1)S(1)}, u32[]{:S(2)}, u32[]{:S(2)}) collective-permute-start(bf16[32,1024]{1,0:T(8,128)(2,1)S(1)} %get-tuple-element.37), channel_id=1, source_target_pairs={{0,8},{4,12},{8,16},{12,20},{16,24},{20,28},{24,0},{28,4},{1,9},{5... | collective-permute-start | bytes 196616 | tf_op jit(solution)/shard_map/ppermute | solution.py:98
  222.1 9.5 %collective-permute-start.7 = (bf16[32,1024]{1,0:T(8,128)(2,1)S(1)}, bf16[32,1024]{1,0:T(8,128)(2,1)S(1)}, u32[]{:S(2)}, u32[]{:S(2)}) collective-permute-start(bf16[32,1024]{1,0:T(8,128)(2,1)S(1)} %get-tuple-element.36), channel_id=1, source_target_pairs={{0,16},{4,20},{8,24},{12,28},{16,0},{20,4},{24,8},{28,12},{1,17},{... | collective-permute-start | bytes 196616 | tf_op jit(solution)/shard_map/ppermute | solution.py:98
  223.3 9.2 %collective-permute-start.8 = (bf16[32,1024]{1,0:T(8,128)(2,1)}, bf16[32,1024]{1,0:T(8,128)(2,1)S(1)}, u32[]{:S(2)}, u32[]{:S(2)}) collective-permute-start(bf16[32,1024]{1,0:T(8,128)(2,1)} %get-tuple-element.35), channel_id=1, source_target_pairs={{0,16},{4,20},{8,24},{12,28},{16,0},{20,4},{24,8},{28,12},{1,17},{... | collective-permute-start | bytes 196616 | tf_op jit(solution)/shard_map/ppermute | solution.py:98
  232.3 6.1 %collective-permute-start.11 = (bf16[32,1024]{1,0:T(8,128)(2,1)S(1)}, bf16[32,1024]{1,0:T(8,128)(2,1)S(1)}, u32[]{:S(2)}, u32[]{:S(2)}) collective-permute-start(bf16[32,1024]{1,0:T(8,128)(2,1)S(1)} %get-tuple-element.40), channel_id=1, source_target_pairs={{0,8},{4,12},{8,16},{12,20},{16,24},{20,28},{24,0},{28,4},{1,9},{5... | collective-permute-start | bytes 196616 | tf_op jit(solution)/shard_map/ppermute | solution.py:98
  233.1 5.9 %collective-permute-start.12 = (bf16[32,1024]{1,0:T(8,128)(2,1)S(1)}, bf16[32,1024]{1,0:T(8,128)(2,1)S(1)}, u32[]{:S(2)}, u32[]{:S(2)}) collective-permute-start(bf16[32,1024]{1,0:T(8,128)(2,1)S(1)} %get-tuple-element.39), channel_id=1, source_target_pairs={{0,24},{4,28},{8,0},{12,4},{16,8},{20,12},{24,16},{28,20},{1,25},{... | collective-permute-start | bytes 196616 | tf_op jit(solution)/shard_map/ppermute | solution.py:98
  239.7 12.3 %all-to-all-start.6 = ((bf16[4,2,32,1024]{3,2,1,0:T(8,128)(2,1)}), bf16[4,2,32,1024]{3,2,1,0:T(8,128)(2,1)S(1)}, u32[]{:S(2)}, u32[]{:S(2)}) async-start(bf16[4,2,32,1024]{3,2,1,0:T(8,128)(2,1)} %bitcast_dynamic-update-slice_fusion.8), calls=%async_computation.6 | async-start | bytes 1048576 | tf_op jit(solution)/shard_map/all_to_all | solution.py:139
  (2 other events, 12.7 us)

commit v4 on v3

--- a/solution.py
+++ b/solution.py
@@ -68,24 +68,27 @@
         basis_mine = jnp.dot(inverse, rows, precision=highest)
         return token_proj, basis_mine
 
-    left = left_stage()
-    weight_sent, grad_sent, left = tie((weight, grad_output, left))
-    other = lax.ppermute(weight_sent, "dp", swap)
+    cut = row_count // 2
+    others = [lax.ppermute(weight[:cut], "dp", swap)]
     low = index % 2 == 0
-    weight_pair = jnp.concatenate(
-        [jnp.where(low, weight, other), jnp.where(low, other, weight)], axis=0
-    )
-    columns = weight_pair.shape[0]
+    columns = 2 * row_count
     piece_rows = half // width
-    upper, under = grad_sent[:half], grad_sent[half:]
+    upper, under = grad_output[:half], grad_output[half:]
     gathered = jnp.zeros((groups, 2, half, grad_output.shape[1]), jnp.bfloat16)
     returned = jnp.zeros((groups, 2, piece_rows, columns), jnp.bfloat16)
 
     def reduced(pieces):
-        product = lax.dot_general(
-            jnp.concatenate(pieces, axis=0), weight_pair, (((1,), (1,)), ((), ())),
-            preferred_element_type=jnp.float32,
-        ).astype(jnp.bfloat16)
+        rows = jnp.concatenate(pieces, axis=0)
+        mine, *rest = (
+            lax.dot_general(
+                rows, part, (((1,), (1,)), ((), ())), preferred_element_type=jnp.float32
+            ).astype(jnp.bfloat16)
+            for part in (weight, *others)
+        )
+        rest = jnp.concatenate(rest, axis=1)
+        product = jnp.concatenate(
+            [jnp.where(low, mine, rest), jnp.where(low, rest, mine)], axis=1
+        )
         product = product.reshape(len(pieces), width, piece_rows, columns).transpose(1, 0, 2, 3)
         parts = lax.all_to_all(product, "tensor", 0, 0, tiled=True)
         return parts.astype(jnp.float32).sum(0).astype(jnp.bfloat16)
@@ -114,13 +117,15 @@
             pieces.append(piece)
         if step + 1 < groups:
             if step == 1:
-                upper, under, token_proj = tie((upper, under, token_proj))
+                left = left_stage()
+                weight_sent, upper, under, left = tie((weight[cut:], upper, under, left))
+                others.append(lax.ppermute(weight_sent, "dp", swap))
             if step == groups - 2:
-                upper, under, weight_pair = tie((upper, under, weight_pair))
+                upper, under, others[1], token_proj = tie((upper, under, others[1], token_proj))
             upper = lax.ppermute(upper, "dp", ahead)
             under = lax.ppermute(under, "dp", behind)
-        if step == 0:
-            token_proj, basis_mine = basis_stage(left)
+            if step == 1:
+                token_proj, basis_mine = basis_stage(left)
     token_proj = spread(token_proj, "dp", along)
 
     rank = start_basis.shape[1]

time: 254 us -> 256 us (level)
  blocking collectives: 14.9 us -> 0 us
  other arithmetic: 30.5 us -> 16.9 us
  local copies, waits for them, and re-layouts: 39.5 us -> 52.4 us
  waiting for transfers between devices: 84.3 us -> 91.6 us
  starting transfers between devices: 52 us -> 58.4 us
  matrix products: 30.6 us -> 34.1 us
    all_to_all x0 -> x1, waiting for transfers between devices: none -> 29.5 us  [left_stage(): left_piece = lax.all_to_all(pieces, 'dp', 0, 0, tiled=True).sum(0)]
    all_to_all x1 -> x0, blocking collectives: 14.9 us -> none  [left_stage(): left_piece = lax.all_to_all(pieces, 'dp', 0, 0, tiled=True).sum(0)]
    all_to_all x5, waiting for transfers between devices: 48.2 us -> 34.3 us  [spread(): lax.all_to_all(copies, axis, 0, 0, axis_index_groups=groups, tiled=True)]
    ppermute x3, waiting for transfers between devices: 28.1 us -> 15.8 us  [body(): under = lax.ppermute(under, 'dp', behind)]
    concatenate x1 -> x2, other arithmetic: 6.68 us -> 0.16 us  [reduced(): jnp.concatenate([jnp.where(low, mine, rest), jnp.where(low, rest, mine)],...]
    select_n x1 -> x0, other arithmetic: 5.47 us -> none  [body(): jnp.where(low, weight, other)]
    dot_general x2 -> x6, matrix products: 15.2 us -> 20.3 us  [reduced(): lax.dot_general(rows, part, (((1,), (1,)), ((), ())), preferred_element_t...]
    slice x1 -> x2, local copies, waits for them, and re-layouts: 2.8 us -> 7.18 us  [the longest x1 4.22 us: body(): others = [lax.ppermute(weight[:cut], 'dp', swap)]]
  transfers between devices with their start and end apart: 22 -> 24, of which waited for: 10 -> 12; matrix products, arithmetic and copies ran while one was open for 30% -> 38% of each run, Pallas kernels for 0% -> 0%
where the time goes in v4:
time: 256 us; the launch traced here: 255 us
  waiting for transfers between devices  91.6 us (36%)
  starting transfers between devices  58.4 us (23%)
  local copies, waits for them, and re-layouts  52.4 us (20%)
  matrix products  34.1 us (13%)
  other arithmetic  16.9 us (7%)
    all_to_all x5, waiting for transfers between devices, spread(): lax.all_to_all(copies, axis, 0, 0, axis_index_groups=groups, tiled=True)  34.3 us
    all_to_all x1, waiting for transfers between devices, left_stage(): left_piece = lax.all_to_all(pieces, 'dp', 0, 0, tiled=True).sum(0)  29.5 us
    dot_general x6, matrix products, reduced(): lax.dot_general(rows, part, (((1,), (1,)), ((), ())), preferred_element_t...  20.3 us
    all_to_all x5, starting transfers between devices, spread(): lax.all_to_all(copies, axis, 0, 0, axis_index_groups=groups, tiled=True)  18 us
    ppermute x3, waiting for transfers between devices, body(): under = lax.ppermute(under, 'dp', behind)  15.8 us
    dynamic_update_slice x8, local copies, waits for them, and re-layouts, body(): lax.dynamic_update_slice(gathered, piece[None, None], (source, place, 0, 0))  13.8 us
    ppermute x6, starting transfers between devices, give_back(): value = lax.ppermute(value, 'dp', back)  8.71 us
    unnamed x22, local copies, waits for them, and re-layouts  8.4 us
  transfers between devices with their start and end apart: 24, of which 12 were waited for; matrix products, arithmetic and copies ran while one was open for 38% of the time, Pallas kernels for 0%

profile of v4, /device:TPU:0, one launch (start us, length us, event | category | flops | bytes accessed | tf_op | source)
XLA Modules:
  0.0 254.6 jit_solution(10040608253638687972)
XLA Ops:
  10.2 3.4 %all-to-all-start = ((f32[4,64,256]{2,1,0:T(8,128)}), f32[4,64,256]{2,1,0:T(8,128)S(1)}, u32[]{:S(2)}, u32[]{:S(2)}) async-start(f32[4,64,256]{2,1,0:T(8,128)} %broadcast_in_dim.81), calls=%async_computation | async-start | bytes 524288 | tf_op jit(solution)/shard_map/all_to_all | solution.py:31
  13.6 4.2 %fusion.54 = (bf16[256,3584]{1,0:T(8,128)(2,1)}, bf16[256,3584]{1,0:T(8,128)(2,1)}) fusion(bf16[512,3584]{1,0:T(8,128)(2,1)} %param.6), kind=kLoop, calls=%fused_computation.120 | loop fusion | bytes 7340032 | tf_op jit(solution)/shard_map/slice | solution.py:72
  19.6 3.7 %broadcast_in_dim.91 = bf16[4,2,128,3584]{3,2,1,0:T(8,128)(2,1)} broadcast(bf16[]{:T(256)} %constant.160.clone.1), dimensions={} | broadcast | bytes 7340034 | tf_op jit(solution)/shard_map/broadcast_in_dim | solution.py:77
  27.4 3.4 %all-to-all-start.1 = ((f32[8,64,128]{2,1,0:T(8,128)}), f32[8,64,128]{2,1,0:T(8,128)S(1)}, u32[]{:S(2)}, u32[]{:S(2)}) async-start(f32[8,64,128]{2,1,0:T(8,128)} %bitcast_bitcast_fusion), calls=%async_computation.1 | async-start | bytes 524288 | tf_op jit(solution)/shard_map/all_to_all | solution.py:54
  33.7 29.5 %all-to-all-done.1 = f32[8,64,128]{2,1,0:T(8,128)S(1)} async-done(((f32[8,64,128]{2,1,0:T(8,128)}), f32[8,64,128]{2,1,0:T(8,128)S(1)}, u32[]{:S(2)}, u32[]{:S(2)}) %all-to-all-start.1) | async-done | bytes 262176 | tf_op jit(solution)/shard_map/all_to_all | solution.py:54
  64.0 4.2 %all-to-all-start.2 = ((f32[8,64,128]{2,1,0:T(8,128)}), f32[8,64,128]{2,1,0:T(8,128)S(1)}, u32[]{:S(2)}, u32[]{:S(2)}) async-start(f32[8,64,128]{2,1,0:T(8,128)} %broadcast_in_dim.82), calls=%async_computation.2 | async-start | bytes 524288 | tf_op jit(solution)/shard_map/all_to_all | solution.py:31
  73.6 3.5 %all-to-all-done.2 = f32[8,64,128]{2,1,0:T(8,128)S(1)} async-done(((f32[8,64,128]{2,1,0:T(8,128)}), f32[8,64,128]{2,1,0:T(8,128)S(1)}, u32[]{:S(2)}, u32[]{:S(2)}) %all-to-all-start.2) | async-done | bytes 262176 | tf_op jit(solution)/shard_map/all_to_all | solution.py:31
  78.7 3.5 %all-to-all-start.3 = ((f32[4,64,320]{2,1,0:T(8,128)}), f32[4,64,320]{2,1,0:T(8,128)S(1)}, u32[]{:S(2)}, u32[]{:S(2)}) async-start(f32[4,64,320]{2,1,0:T(8,128)} %broadcast_in_dim.83), calls=%async_computation.3 | async-start | bytes 786432 | tf_op jit(solution)/shard_map/all_to_all | solution.py:31
  90.4 3.5 %all-to-all-start.8 = ((f32[4,64,512]{2,1,0:T(8,128)}), f32[4,64,512]{2,1,0:T(8,128)S(1)}, u32[]{:S(2)}, u32[]{:S(2)}) async-start(f32[4,64,512]{2,1,0:T(8,128)} %broadcast_in_dim.100), calls=%async_computation.8 | async-start | bytes 1048576 | tf_op jit(solution)/shard_map/all_to_all | solution.py:31
  94.0 5.8 %cholesky.17 = f32[64,64]{1,0:T(8,128)S(1)} custom-call(f32[64,64]{1,0:T(8,128)S(1)} %fusion.45), custom_call_target="Cholesky" | custom-call | tf_op jit(solution)/shard_map/jit(cholesky)/cholesky | solution.py:62
  101.2 4.9 %custom-call.7 = f32[1,64,64]{1,2,0:T(8,128)S(1)} custom-call(f32[1,64,64]{2,1,0:T(8,128)S(1)} %fusion.42), custom_call_target="InvertDiagBlocksLowerTriangular" | custom-call | tf_op jit(solution)/shard_map/jit(_solve_triangular)/triangular_solve | solution.py:63
  110.6 15.8 %collective-permute-done.3 = bf16[128,3584]{1,0:T(8,128)(2,1)} collective-permute-done((bf16[128,3584]{1,0:T(8,128)(2,1)S(1)}, bf16[128,3584]{1,0:T(8,128)(2,1)}, u32[]{:S(2)}, u32[]{:S(2)}) %collective-permute-start.3) | collective-permute-done | bytes 917536 | tf_op jit(solution)/shard_map/ppermute | solution.py:126
  128.6 4.9 %convolution_convert_fusion.2 = bf16[768,256]{0,1:T(8,128)(2,1)S(1)} fusion(bf16[768,3584]{1,0:T(8,128)(2,1)} %constant_dynamic-update-slice_fusion, bf16[256,3584]{1,0:T(8,128)(2,1)} %collective-permute-done.4), kind=kOutput, calls=%fused_computation.11 | convolution fusion | flops 1409482752 | bytes 7733248 | tf_op jit(solution)/shard_map/dot_general | solution.py:83
  137.8 3.1 %convolution_convert_fusion.1 = bf16[768,256]{0,1:T(8,128)(2,1)S(1)} fusion(bf16[768,3584]{1,0:T(8,128)(2,1)S(1)} %copy-done.6, bf16[256,3584]{1,0:T(8,128)(2,1)} %collective-permute-done.5), kind=kOutput, calls=%fused_computation.10 | convolution fusion | flops 1409482752 | bytes 7733248 | tf_op jit(solution)/shard_map/dot_general | solution.py:83
  141.5 3.3 %collective-permute-start.11 = (bf16[128,3584]{1,0:T(8,128)(2,1)}, bf16[128,3584]{1,0:T(8,128)(2,1)}, u32[]{:S(2)}, u32[]{:S(2)}) collective-permute-start(bf16[128,3584]{1,0:T(8,128)(2,1)} %collective-permute-done.3), channel_id=1, source_target_pairs={{0,24},{4,28},{8,0},{12,4},{16,8},{20,12},{24,16},{28,20},{1,25},{... | collective-permute-start | bytes 2752520 | tf_op jit(solution)/shard_map/ppermute | solution.py:126
  145.5 3.4 %all-to-all-start.7 = ((f32[4,64,256]{2,1,0:T(8,128)}), f32[4,64,256]{2,1,0:T(8,128)S(1)}, u32[]{:S(2)}, u32[]{:S(2)}) async-start(f32[4,64,256]{2,1,0:T(8,128)} %broadcast_in_dim.90), calls=%async_computation.7 | async-start | bytes 524288 | tf_op jit(solution)/shard_map/all_to_all | solution.py:31
  149.0 6.7 %broadcast_select_fusion.1 = (bf16[768,512]{0,1:T(8,128)(2,1)S(1)}, bf16[768,512]{0,1:T(8,128)(2,1)S(1)}) fusion(pred[]{:T(512)S(6)} %eq.23, bf16[768,256]{0,1:T(8,128)(2,1)S(1)} %convolution_convert_fusion.1, bf16[768,256]{0,1:T(8,128)(2,1)S(1)} %convolution_convert_fusion.2, bf16[768,3584]{1,0:T(8,128)(2,1)} %constant_dynamic-update-slice_fusion, ...), kind=kOutput, calls=%fused_computation.35 | convolution fusion | flops 2821324800 | bytes 11534337 | tf_op jit(solution)/shard_map/dot_general | solution.py:83
  160.3 29.6 %all-to-all-done.7 = f32[4,64,256]{2,1,0:T(8,128)S(1)} async-done(((f32[4,64,256]{2,1,0:T(8,128)}), f32[4,64,256]{2,1,0:T(8,128)S(1)}, u32[]{:S(2)}, u32[]{:S(2)}) %all-to-all-start.7) | async-done | bytes 262176 | tf_op jit(solution)/shard_map/all_to_all | solution.py:31
  189.9 4.5 %all-to-all-start.4 = ((bf16[4,6,32,1024]{3,2,1,0:T(8,128)(2,1)}), bf16[4,6,32,1024]{3,2,1,0:T(8,128)(2,1)}, u32[]{:S(2)}, u32[]{:S(2)}) async-start(bf16[4,6,32,1024]{3,2,1,0:T(8,128)(2,1)} %copy.34), calls=%async_computation.4 | async-start | bytes 3145728 | tf_op jit(solution)/shard_map/all_to_all | solution.py:93
  205.5 4.2 %fusion.21 = f32[128,3584]{1,0:T(8,128)S(1)} fusion(bf16[1024,3584]{1,0:T(8,128)(2,1)} %bitcast.39, bf16[64,1024]{1,0:T(8,128)(2,1)S(1)} %get-tuple-element.21, bf16[64,1024]{1,0:T(8,128)(2,1)S(1)} %get-tuple-element.22), kind=kOutput, calls=%fused_computation.50 | convolution fusion | flops 940048384 | bytes 9437184 | tf_op jit(solution)/shard_map/dot_general | solution.py:19
  214.4 3.5 %all-to-all-start.5 = ((bf16[4,2,32,1024]{3,2,1,0:T(8,128)(2,1)}), bf16[4,2,32,1024]{3,2,1,0:T(8,128)(2,1)S(1)}, u32[]{:S(2)}, u32[]{:S(2)}) async-start(bf16[4,2,32,1024]{3,2,1,0:T(8,128)(2,1)} %bitcast.120), calls=%async_computation.5 | async-start | bytes 1048576 | tf_op jit(solution)/shard_map/all_to_all | solution.py:93
  234.9 3.7 %collective-permute-start.13 = (bf16[32,1024]{1,0:T(8,128)(2,1)S(1)}, bf16[32,1024]{1,0:T(8,128)(2,1)S(1)}, u32[]{:S(2)}, u32[]{:S(2)}) collective-permute-start(bf16[32,1024]{1,0:T(8,128)(2,1)S(1)} %get-tuple-element.41), channel_id=1, source_target_pairs={{0,24},{4,28},{8,0},{12,4},{16,8},{20,12},{24,16},{28,20},{1,25},{... | collective-permute-start | bytes 196616 | tf_op jit(solution)/shard_map/ppermute | solution.py:101
  241.4 3.5 %all-to-all-start.6 = ((bf16[4,2,32,1024]{3,2,1,0:T(8,128)(2,1)}), bf16[4,2,32,1024]{3,2,1,0:T(8,128)(2,1)S(1)}, u32[]{:S(2)}, u32[]{:S(2)}) async-start(bf16[4,2,32,1024]{3,2,1,0:T(8,128)(2,1)} %bitcast_dynamic-update-slice_fusion.8), calls=%async_computation.6 | async-start | bytes 1048576 | tf_op jit(solution)/shard_map/all_to_all | solution.py:144
  246.0 6.7 %multiply_subtract_fusion = f32[512,3584]{1,0:T(8,128)} fusion(bf16[512,3584]{1,0:T(8,128)(2,1)} %param.6, bf16[64,3584]{1,0:T(8,128)(2,1)S(1)} %collective-permute-done.14, bf16[64,3584]{1,0:T(8,128)(2,1)} %fusion.7, bf16[64,512]{1,0:T(8,128)(2,1)S(1)} %get-tuple-element.19, bf16[64,512]{1,0:T(8,128)(2,1)S(1)} %copy-done.7), kind=kOutput, calls=%fused_computation | convolution fusion | flops 953417728 | bytes 12058624 | tf_op jit(solution)/shard_map/dot_general | solution.py:148
  (121 shorter events, 90.9 us)
Async XLA Ops:
  3.6 64.6 %collective-permute-start = (bf16[128,3584]{1,0:T(8,128)(2,1)}, bf16[128,3584]{1,0:T(8,128)(2,1)}, u32[]{:S(2)}, u32[]{:S(2)}) collective-permute-start(bf16[128,3584]{1,0:T(8,128)(2,1)} %get-tuple-element.32), channel_id=1, source_target_pairs={{0,8},{4,12},{8,16},{12,20},{16,24},{20,28},{24,0},{28,4},{1,9},{5... | collective-permute-start | bytes 2752520 | tf_op jit(solution)/shard_map/ppermute | solution.py:125
  6.7 63.8 %collective-permute-start.1 = (bf16[128,3584]{1,0:T(8,128)(2,1)}, bf16[128,3584]{1,0:T(8,128)(2,1)S(1)}, u32[]{:S(2)}, u32[]{:S(2)}) collective-permute-start(bf16[128,3584]{1,0:T(8,128)(2,1)} %get-tuple-element.31), channel_id=1, source_target_pairs={{0,24},{4,28},{8,0},{12,4},{16,8},{20,12},{24,16},{28,20},{1,25},{... | collective-permute-start | bytes 2752520 | tf_op jit(solution)/shard_map/ppermute | solution.py:126
  10.2 16.2 %all-to-all-start = ((f32[4,64,256]{2,1,0:T(8,128)}), f32[4,64,256]{2,1,0:T(8,128)S(1)}, u32[]{:S(2)}, u32[]{:S(2)}) async-start(f32[4,64,256]{2,1,0:T(8,128)} %broadcast_in_dim.81), calls=%async_computation | async-start | bytes 524288 | tf_op jit(solution)/shard_map/all_to_all | solution.py:31
  17.9 110.7 %collective-permute-start.4 = (bf16[256,3584]{1,0:T(8,128)(2,1)}, bf16[256,3584]{1,0:T(8,128)(2,1)}, u32[]{:S(2)}, u32[]{:S(2)}) collective-permute-start(bf16[256,3584]{1,0:T(8,128)(2,1)} %get-tuple-element.29), channel_id=1, source_target_pairs={{0,4},{4,0},{8,12},{12,8},{16,20},{20,16},{24,28},{28,24},{1,5},{5... | collective-permute-start | bytes 5505032 | tf_op jit(solution)/shard_map/ppermute | solution.py:72
  27.4 35.8 %all-to-all-start.1 = ((f32[8,64,128]{2,1,0:T(8,128)}), f32[8,64,128]{2,1,0:T(8,128)S(1)}, u32[]{:S(2)}, u32[]{:S(2)}) async-start(f32[8,64,128]{2,1,0:T(8,128)} %bitcast_bitcast_fusion), calls=%async_computation.1 | async-start | bytes 524288 | tf_op jit(solution)/shard_map/all_to_all | solution.py:54
  64.0 13.1 %all-to-all-start.2 = ((f32[8,64,128]{2,1,0:T(8,128)}), f32[8,64,128]{2,1,0:T(8,128)S(1)}, u32[]{:S(2)}, u32[]{:S(2)}) async-start(f32[8,64,128]{2,1,0:T(8,128)} %broadcast_in_dim.82), calls=%async_computation.2 | async-start | bytes 524288 | tf_op jit(solution)/shard_map/all_to_all | solution.py:31
  78.7 10.9 %all-to-all-start.3 = ((f32[4,64,320]{2,1,0:T(8,128)}), f32[4,64,320]{2,1,0:T(8,128)S(1)}, u32[]{:S(2)}, u32[]{:S(2)}) async-start(f32[4,64,320]{2,1,0:T(8,128)} %broadcast_in_dim.83), calls=%async_computation.3 | async-start | bytes 786432 | tf_op jit(solution)/shard_map/all_to_all | solution.py:31
  83.1 25.3 %collective-permute-start.2 = (bf16[128,3584]{1,0:T(8,128)(2,1)}, bf16[128,3584]{1,0:T(8,128)(2,1)}, u32[]{:S(2)}, u32[]{:S(2)}) collective-permute-start(bf16[128,3584]{1,0:T(8,128)(2,1)} %collective-permute-done), channel_id=1, source_target_pairs={{0,8},{4,12},{8,16},{12,20},{16,24},{20,28},{24,0},{28,4},{1,9},{5... | collective-permute-start | bytes 2752520 | tf_op jit(solution)/shard_map/ppermute | solution.py:125
  84.2 42.2 %collective-permute-start.3 = (bf16[128,3584]{1,0:T(8,128)(2,1)S(1)}, bf16[128,3584]{1,0:T(8,128)(2,1)}, u32[]{:S(2)}, u32[]{:S(2)}) collective-permute-start(bf16[128,3584]{1,0:T(8,128)(2,1)S(1)} %collective-permute-done.1), channel_id=1, source_target_pairs={{0,24},{4,28},{8,0},{12,4},{16,8},{20,12},{24,16},{28,20},{1,25},{... | collective-permute-start | bytes 2752520 | tf_op jit(solution)/shard_map/ppermute | solution.py:126
  87.0 50.9 %collective-permute-start.5 = (bf16[256,3584]{1,0:T(8,128)(2,1)}, bf16[256,3584]{1,0:T(8,128)(2,1)}, u32[]{:S(2)}, u32[]{:S(2)}) collective-permute-start(bf16[256,3584]{1,0:T(8,128)(2,1)} %get-tuple-element.13), channel_id=1, source_target_pairs={{0,4},{4,0},{8,12},{12,8},{16,20},{20,16},{24,28},{28,24},{1,5},{5... | collective-permute-start | bytes 5505032 | tf_op jit(solution)/shard_map/ppermute | solution.py:122
  90.4 16.1 %all-to-all-start.8 = ((f32[4,64,512]{2,1,0:T(8,128)}), f32[4,64,512]{2,1,0:T(8,128)S(1)}, u32[]{:S(2)}, u32[]{:S(2)}) async-start(f32[4,64,512]{2,1,0:T(8,128)} %broadcast_in_dim.100), calls=%async_computation.8 | async-start | bytes 1048576 | tf_op jit(solution)/shard_map/all_to_all | solution.py:31
  140.9 53.5 %collective-permute-start.10 = (bf16[128,3584]{1,0:T(8,128)(2,1)}, bf16[128,3584]{1,0:T(8,128)(2,1)S(1)}, u32[]{:S(2)}, u32[]{:S(2)}) collective-permute-start(bf16[128,3584]{1,0:T(8,128)(2,1)} %collective-permute-done.2), channel_id=1, source_target_pairs={{0,8},{4,12},{8,16},{12,20},{16,24},{20,28},{24,0},{28,4},{1,9},{5... | collective-permute-start | bytes 2752520 | tf_op jit(solution)/shard_map/ppermute | solution.py:125
  141.5 53.0 %collective-permute-start.11 = (bf16[128,3584]{1,0:T(8,128)(2,1)}, bf16[128,3584]{1,0:T(8,128)(2,1)}, u32[]{:S(2)}, u32[]{:S(2)}) collective-permute-start(bf16[128,3584]{1,0:T(8,128)(2,1)} %collective-permute-done.3), channel_id=1, source_target_pairs={{0,24},{4,28},{8,0},{12,4},{16,8},{20,12},{24,16},{28,20},{1,25},{... | collective-permute-start | bytes 2752520 | tf_op jit(solution)/shard_map/ppermute | solution.py:126
  145.5 44.4 %all-to-all-start.7 = ((f32[4,64,256]{2,1,0:T(8,128)}), f32[4,64,256]{2,1,0:T(8,128)S(1)}, u32[]{:S(2)}, u32[]{:S(2)}) async-start(f32[4,64,256]{2,1,0:T(8,128)} %broadcast_in_dim.90), calls=%async_computation.7 | async-start | bytes 524288 | tf_op jit(solution)/shard_map/all_to_all | solution.py:31
  189.9 24.5 %all-to-all-start.4 = ((bf16[4,6,32,1024]{3,2,1,0:T(8,128)(2,1)}), bf16[4,6,32,1024]{3,2,1,0:T(8,128)(2,1)}, u32[]{:S(2)}, u32[]{:S(2)}) async-start(bf16[4,6,32,1024]{3,2,1,0:T(8,128)(2,1)} %copy.34), calls=%async_computation.4 | async-start | bytes 3145728 | tf_op jit(solution)/shard_map/all_to_all | solution.py:93
  210.6 34.3 %collective-permute-start.14 = (bf16[64,3584]{1,0:T(8,128)(2,1)}, bf16[64,3584]{1,0:T(8,128)(2,1)S(1)}, u32[]{:S(2)}, u32[]{:S(2)}) collective-permute-start(bf16[64,3584]{1,0:T(8,128)(2,1)} %fusion.7), channel_id=1, source_target_pairs={{0,4},{4,0},{8,12},{12,8},{16,20},{20,16},{24,28},{28,24},{1,5},{5... | collective-permute-start | bytes 1376264 | tf_op jit(solution)/shard_map/ppermute | solution.py:137
  214.4 19.6 %all-to-all-start.5 = ((bf16[4,2,32,1024]{3,2,1,0:T(8,128)(2,1)}), bf16[4,2,32,1024]{3,2,1,0:T(8,128)(2,1)S(1)}, u32[]{:S(2)}, u32[]{:S(2)}) async-start(bf16[4,2,32,1024]{3,2,1,0:T(8,128)(2,1)} %bitcast.120), calls=%async_computation.5 | async-start | bytes 1048576 | tf_op jit(solution)/shard_map/all_to_all | solution.py:93
  221.1 5.6 %collective-permute-start.6 = (bf16[32,1024]{1,0:T(8,128)(2,1)S(1)}, bf16[32,1024]{1,0:T(8,128)(2,1)S(1)}, u32[]{:S(2)}, u32[]{:S(2)}) collective-permute-start(bf16[32,1024]{1,0:T(8,128)(2,1)S(1)} %get-tuple-element.40), channel_id=1, source_target_pairs={{0,24},{4,28},{8,0},{12,4},{16,8},{20,12},{24,16},{28,20},{1,25},{... | collective-permute-start | bytes 196616 | tf_op jit(solution)/shard_map/ppermute | solution.py:101
  223.0 6.8 %collective-permute-start.7 = (bf16[32,1024]{1,0:T(8,128)(2,1)S(1)}, bf16[32,1024]{1,0:T(8,128)(2,1)S(1)}, u32[]{:S(2)}, u32[]{:S(2)}) collective-permute-start(bf16[32,1024]{1,0:T(8,128)(2,1)S(1)} %get-tuple-element.39), channel_id=1, source_target_pairs={{0,8},{4,12},{8,16},{12,20},{16,24},{20,28},{24,0},{28,4},{1,9},{5... | collective-permute-start | bytes 196616 | tf_op jit(solution)/shard_map/ppermute | solution.py:101
  223.8 9.5 %collective-permute-start.8 = (bf16[32,1024]{1,0:T(8,128)(2,1)S(1)}, bf16[32,1024]{1,0:T(8,128)(2,1)S(1)}, u32[]{:S(2)}, u32[]{:S(2)}) collective-permute-start(bf16[32,1024]{1,0:T(8,128)(2,1)S(1)} %get-tuple-element.38), channel_id=1, source_target_pairs={{0,16},{4,20},{8,24},{12,28},{16,0},{20,4},{24,8},{28,12},{1,17},{... | collective-permute-start | bytes 196616 | tf_op jit(solution)/shard_map/ppermute | solution.py:101
  223.8 10.4 %collective-permute-start.9 = (bf16[32,1024]{1,0:T(8,128)(2,1)S(1)}, bf16[32,1024]{1,0:T(8,128)(2,1)S(1)}, u32[]{:S(2)}, u32[]{:S(2)}) collective-permute-start(bf16[32,1024]{1,0:T(8,128)(2,1)S(1)} %get-tuple-element.37), channel_id=1, source_target_pairs={{0,16},{4,20},{8,24},{12,28},{16,0},{20,4},{24,8},{28,12},{1,17},{... | collective-permute-start | bytes 196616 | tf_op jit(solution)/shard_map/ppermute | solution.py:101
  234.0 6.1 %collective-permute-start.12 = (bf16[32,1024]{1,0:T(8,128)(2,1)S(1)}, bf16[32,1024]{1,0:T(8,128)(2,1)S(1)}, u32[]{:S(2)}, u32[]{:S(2)}) collective-permute-start(bf16[32,1024]{1,0:T(8,128)(2,1)S(1)} %get-tuple-element.42), channel_id=1, source_target_pairs={{0,8},{4,12},{8,16},{12,20},{16,24},{20,28},{24,0},{28,4},{1,9},{5... | collective-permute-start | bytes 196616 | tf_op jit(solution)/shard_map/ppermute | solution.py:101
  234.9 5.9 %collective-permute-start.13 = (bf16[32,1024]{1,0:T(8,128)(2,1)S(1)}, bf16[32,1024]{1,0:T(8,128)(2,1)S(1)}, u32[]{:S(2)}, u32[]{:S(2)}) collective-permute-start(bf16[32,1024]{1,0:T(8,128)(2,1)S(1)} %get-tuple-element.41), channel_id=1, source_target_pairs={{0,24},{4,28},{8,0},{12,4},{16,8},{20,12},{24,16},{28,20},{1,25},{... | collective-permute-start | bytes 196616 | tf_op jit(solution)/shard_map/ppermute | solution.py:101
  241.4 12.3 %all-to-all-start.6 = ((bf16[4,2,32,1024]{3,2,1,0:T(8,128)(2,1)}), bf16[4,2,32,1024]{3,2,1,0:T(8,128)(2,1)S(1)}, u32[]{:S(2)}, u32[]{:S(2)}) async-start(bf16[4,2,32,1024]{3,2,1,0:T(8,128)(2,1)} %bitcast_dynamic-update-slice_fusion.8), calls=%async_computation.6 | async-start | bytes 1048576 | tf_op jit(solution)/shard_map/all_to_all | solution.py:144
  (8 other events, 94.3 us)

commit v5 on v4

--- a/solution.py
+++ b/solution.py
@@ -68,7 +68,8 @@
         basis_mine = jnp.dot(inverse, rows, precision=highest)
         return token_proj, basis_mine
 
-    cut = row_count // 2
+    cut = row_count // 4
+    own = weight
     others = [lax.ppermute(weight[:cut], "dp", swap)]
     low = index % 2 == 0
     columns = 2 * row_count
@@ -83,7 +84,7 @@
             lax.dot_general(
                 rows, part, (((1,), (1,)), ((), ())), preferred_element_type=jnp.float32
             ).astype(jnp.bfloat16)
-            for part in (weight, *others)
+            for part in (own, *others)
         )
         rest = jnp.concatenate(rest, axis=1)
         product = jnp.concatenate(
@@ -109,6 +110,7 @@
             total = reduced(pieces)
             for earlier in range(step):
                 returned = give_back(returned, total[2 * earlier : 2 * earlier + 2], earlier)
+            upper, under, returned = tie((upper, under, returned))
             total = reduced([upper, under])
             returned = give_back(returned, total, step)
         sources = ((group - step + groups) % groups, (group + step) % groups)
@@ -121,13 +123,14 @@
                 weight_sent, upper, under, left = tie((weight[cut:], upper, under, left))
                 others.append(lax.ppermute(weight_sent, "dp", swap))
             if step == groups - 2:
-                upper, under, others[1], token_proj = tie((upper, under, others[1], token_proj))
+                upper, under, own, others[0], token_proj = tie(
+                    (upper, under, own, others[0], token_proj)
+                )
             upper = lax.ppermute(upper, "dp", ahead)
             under = lax.ppermute(under, "dp", behind)
             if step == 1:
                 token_proj, basis_mine = basis_stage(left)
-    token_proj = spread(token_proj, "dp", along)
-
+                token_proj = spread(token_proj, "dp", along)
     rank = start_basis.shape[1]
     right_part = thin_product(
         token_proj.transpose(1, 0, 2).reshape(rank, groups * tokens),

time: 256 us -> 257 us (level)
  waiting for transfers between devices: 91.6 us -> 94.6 us
    all_to_all x2, waiting for transfers between devices: 2.85 us -> 23.7 us  [reduced(): parts = lax.all_to_all(product, 'tensor', 0, 0, tiled=True)]
    ppermute x3, waiting for transfers between devices: 15.8 us -> 0.01 us  [body(): under = lax.ppermute(under, 'dp', behind)]
    all_to_all x5, waiting for transfers between devices: 34.3 us -> 29.4 us  [spread(): lax.all_to_all(copies, axis, 0, 0, axis_index_groups=groups, tiled=True)]
    slice x0 -> x1, local copies, waits for them, and re-layouts: none -> 3.57 us  [body(): weight_sent, upper, under, left = tie((weight[cut:], upper, under, left))]
    ppermute x1, waiting for transfers between devices: 0.01 us -> 3.21 us  [body(): others.append(lax.ppermute(weight_sent, 'dp', swap))]
    ppermute x1, waiting for transfers between devices: 0.01 us -> 3.07 us  [body(): right_other = lax.ppermute(right_part, 'dp', swap)]
    unnamed x22 -> x24, local copies, waits for them, and re-layouts: 8.4 us -> 8.4 us
  transfers between devices with their start and end apart: 24 -> 24, of which waited for: 12 -> 13; matrix products, arithmetic and copies ran while one was open for 38% -> 38% of each run, Pallas kernels for 0% -> 0%
where the time goes in v5:
time: 257 us; the launch traced here: 256 us
  waiting for transfers between devices  94.6 us (37%)
  starting transfers between devices  56.3 us (22%)
  local copies, waits for them, and re-layouts  52.6 us (20%)
  matrix products  32.9 us (13%)
  other arithmetic  18.5 us (7%)
    all_to_all x5, waiting for transfers between devices, spread(): lax.all_to_all(copies, axis, 0, 0, axis_index_groups=groups, tiled=True)  29.4 us
    all_to_all x1, waiting for transfers between devices, left_stage(): left_piece = lax.all_to_all(pieces, 'dp', 0, 0, tiled=True).sum(0)  27.1 us
    all_to_all x2, waiting for transfers between devices, reduced(): parts = lax.all_to_all(product, 'tensor', 0, 0, tiled=True)  23.7 us
    all_to_all x5, starting transfers between devices, spread(): lax.all_to_all(copies, axis, 0, 0, axis_index_groups=groups, tiled=True)  18.5 us
    dot_general x6, matrix products, reduced(): lax.dot_general(rows, part, (((1,), (1,)), ((), ())), preferred_element_t...  17.9 us
    dynamic_update_slice x8, local copies, waits for them, and re-layouts, body(): lax.dynamic_update_slice(gathered, piece[None, None], (source, place, 0, 0))  12.6 us
    ppermute x3, starting transfers between devices, body(): under = lax.ppermute(under, 'dp', behind)  9.07 us
    unnamed x24, local copies, waits for them, and re-layouts  8.4 us
  transfers between devices with their start and end apart: 24, of which 13 were waited for; matrix products, arithmetic and copies ran while one was open for 38% of the time, Pallas kernels for 0%

profile of v5, /device:TPU:0, one launch (start us, length us, event | category | flops | bytes accessed | tf_op | source)
XLA Modules:
  0.0 256.0 jit_solution(13212458896603110898)
XLA Ops:
  5.0 4.2 %all-to-all-start = ((f32[4,64,256]{2,1,0:T(8,128)}), f32[4,64,256]{2,1,0:T(8,128)S(1)}, u32[]{:S(2)}, u32[]{:S(2)}) async-start(f32[4,64,256]{2,1,0:T(8,128)} %broadcast_in_dim.80), calls=%async_computation | async-start | bytes 524288 | tf_op jit(solution)/shard_map/all_to_all | solution.py:31
  16.4 3.6 %collective-permute-start.1 = (bf16[128,3584]{1,0:T(8,128)(2,1)}, bf16[128,3584]{1,0:T(8,128)(2,1)S(1)}, u32[]{:S(2)}, u32[]{:S(2)}) collective-permute-start(bf16[128,3584]{1,0:T(8,128)(2,1)} %get-tuple-element.37), channel_id=1, source_target_pairs={{0,24},{4,28},{8,0},{12,4},{16,8},{20,12},{24,16},{28,20},{1,25},{... | collective-permute-start | bytes 2752520 | tf_op jit(solution)/shard_map/ppermute | solution.py:130
  20.0 3.7 %broadcast_in_dim.91 = bf16[4,2,128,3584]{3,2,1,0:T(8,128)(2,1)} broadcast(bf16[]{:T(256)} %constant.168.clone.1), dimensions={} | broadcast | bytes 7340034 | tf_op jit(solution)/shard_map/broadcast_in_dim | solution.py:78
  25.6 3.6 %slice.88 = bf16[384,3584]{1,0:T(8,128)(2,1)} slice(bf16[512,3584]{1,0:T(8,128)(2,1)} %param.6), slice={[128:512], [0:3584]} | slice | bytes 5505024 | tf_op jit(solution)/shard_map/slice | solution.py:123
  30.2 5.1 %all-to-all-start.1 = ((f32[8,64,128]{2,1,0:T(8,128)}), f32[8,64,128]{2,1,0:T(8,128)S(1)}, u32[]{:S(2)}, u32[]{:S(2)}) async-start(f32[8,64,128]{2,1,0:T(8,128)} %bitcast_bitcast_fusion), calls=%async_computation.1 | async-start | bytes 524288 | tf_op jit(solution)/shard_map/all_to_all | solution.py:54
  38.2 27.1 %all-to-all-done.1 = f32[8,64,128]{2,1,0:T(8,128)S(1)} async-done(((f32[8,64,128]{2,1,0:T(8,128)}), f32[8,64,128]{2,1,0:T(8,128)S(1)}, u32[]{:S(2)}, u32[]{:S(2)}) %all-to-all-start.1) | async-done | bytes 262176 | tf_op jit(solution)/shard_map/all_to_all | solution.py:54
  66.1 4.0 %all-to-all-start.2 = ((f32[8,64,128]{2,1,0:T(8,128)}), f32[8,64,128]{2,1,0:T(8,128)S(1)}, u32[]{:S(2)}, u32[]{:S(2)}) async-start(f32[8,64,128]{2,1,0:T(8,128)} %broadcast_in_dim.81), calls=%async_computation.2 | async-start | bytes 524288 | tf_op jit(solution)/shard_map/all_to_all | solution.py:31
  73.2 5.1 %all-to-all-done.2 = f32[8,64,128]{2,1,0:T(8,128)S(1)} async-done(((f32[8,64,128]{2,1,0:T(8,128)}), f32[8,64,128]{2,1,0:T(8,128)S(1)}, u32[]{:S(2)}, u32[]{:S(2)}) %all-to-all-start.2) | async-done | bytes 262176 | tf_op jit(solution)/shard_map/all_to_all | solution.py:31
  79.8 3.5 %all-to-all-start.3 = ((f32[4,64,320]{2,1,0:T(8,128)}), f32[4,64,320]{2,1,0:T(8,128)S(1)}, u32[]{:S(2)}, u32[]{:S(2)}) async-start(f32[4,64,320]{2,1,0:T(8,128)} %broadcast_in_dim.82), calls=%async_computation.3 | async-start | bytes 786432 | tf_op jit(solution)/shard_map/all_to_all | solution.py:31
  85.6 3.7 %collective-permute-start.3 = (bf16[128,3584]{1,0:T(8,128)(2,1)S(1)}, bf16[128,3584]{1,0:T(8,128)(2,1)}, u32[]{:S(2)}, u32[]{:S(2)}) collective-permute-start(bf16[128,3584]{1,0:T(8,128)(2,1)S(1)} %collective-permute-done.1), channel_id=1, source_target_pairs={{0,24},{4,28},{8,0},{12,4},{16,8},{20,12},{24,16},{28,20},{1,25},{... | collective-permute-start | bytes 2752520 | tf_op jit(solution)/shard_map/ppermute | solution.py:130
  90.8 5.8 %cholesky.17 = f32[64,64]{1,0:T(8,128)S(1)} custom-call(f32[64,64]{1,0:T(8,128)S(1)} %fusion.45), custom_call_target="Cholesky" | custom-call | tf_op jit(solution)/shard_map/jit(cholesky)/cholesky | solution.py:62
  98.0 4.9 %custom-call.7 = f32[1,64,64]{1,2,0:T(8,128)S(1)} custom-call(f32[1,64,64]{2,1,0:T(8,128)S(1)} %fusion.42), custom_call_target="InvertDiagBlocksLowerTriangular" | custom-call | tf_op jit(solution)/shard_map/jit(_solve_triangular)/triangular_solve | solution.py:63
  108.5 24.1 %all-to-all-done.4 = f32[4,64,256]{2,1,0:T(8,128)S(1)} async-done(((f32[4,64,256]{2,1,0:T(8,128)}), f32[4,64,256]{2,1,0:T(8,128)S(1)}, u32[]{:S(2)}, u32[]{:S(2)}) %all-to-all-start.4) | async-done | bytes 262176 | tf_op jit(solution)/shard_map/all_to_all | solution.py:31
  140.9 4.8 %convolution_convert_fusion.4 = bf16[768,128]{0,1:T(8,128)(2,1)S(1)} fusion(bf16[768,3584]{1,0:T(8,128)(2,1)} %constant_dynamic-update-slice_fusion, bf16[128,3584]{1,0:T(8,128)(2,1)} %collective-permute-done.4), kind=kOutput, calls=%fused_computation.13 | convolution fusion | flops 704741376 | bytes 6619136 | tf_op jit(solution)/shard_map/dot_general | solution.py:84
  151.1 4.1 %convolution_convert_fusion.1 = bf16[768,384]{0,1:T(8,128)(2,1)S(1)} fusion(bf16[768,3584]{1,0:T(8,128)(2,1)S(1)} %copy-done.5, bf16[384,3584]{1,0:T(8,128)(2,1)} %collective-permute-done.7), kind=kOutput, calls=%fused_computation.10 | convolution fusion | flops 2114224128 | bytes 8847360 | tf_op jit(solution)/shard_map/dot_general | solution.py:84
  162.8 3.6 %all-to-all-start.5 = ((bf16[4,6,32,1024]{3,2,1,0:T(8,128)(2,1)}), bf16[4,6,32,1024]{3,2,1,0:T(8,128)(2,1)S(1)}, u32[]{:S(2)}, u32[]{:S(2)}) async-start(bf16[4,6,32,1024]{3,2,1,0:T(8,128)(2,1)} %copy.30), calls=%async_computation.5 | async-start | bytes 3145728 | tf_op jit(solution)/shard_map/all_to_all | solution.py:94
  169.2 17.2 %all-to-all-done.5 = bf16[4,6,32,1024]{3,2,1,0:T(8,128)(2,1)S(1)} async-done(((bf16[4,6,32,1024]{3,2,1,0:T(8,128)(2,1)}), bf16[4,6,32,1024]{3,2,1,0:T(8,128)(2,1)S(1)}, u32[]{:S(2)}, u32[]{:S(2)}) %all-to-all-start.5) | async-done | bytes 1572896 | tf_op jit(solution)/shard_map/all_to_all | solution.py:94
  187.3 3.5 %all-to-all-start.8 = ((f32[4,64,512]{2,1,0:T(8,128)}), f32[4,64,512]{2,1,0:T(8,128)S(1)}, u32[]{:S(2)}, u32[]{:S(2)}) async-start(f32[4,64,512]{2,1,0:T(8,128)} %broadcast_in_dim.100), calls=%async_computation.8 | async-start | bytes 1048576 | tf_op jit(solution)/shard_map/all_to_all | solution.py:31
  198.9 4.3 %collective-permute-done.9 = bf16[32,1024]{1,0:T(8,128)(2,1)S(1)} collective-permute-done((bf16[32,1024]{1,0:T(8,128)(2,1)S(1)}, bf16[32,1024]{1,0:T(8,128)(2,1)S(1)}, u32[]{:S(2)}, u32[]{:S(2)}) %collective-permute-start.9) | collective-permute-done | bytes 65568 | tf_op jit(solution)/shard_map/ppermute | solution.py:102
  216.9 4.2 %fusion.21 = f32[128,3584]{1,0:T(8,128)S(1)} fusion(bf16[1024,3584]{1,0:T(8,128)(2,1)} %bitcast.39, bf16[64,1024]{1,0:T(8,128)(2,1)S(1)} %get-tuple-element.29, bf16[64,1024]{1,0:T(8,128)(2,1)S(1)} %copy-done.6), kind=kOutput, calls=%fused_computation.50 | convolution fusion | flops 940048384 | bytes 9437184 | tf_op jit(solution)/shard_map/dot_general | solution.py:19
  221.2 3.5 %all-to-all-start.6 = ((bf16[4,2,32,1024]{3,2,1,0:T(8,128)(2,1)}), bf16[4,2,32,1024]{3,2,1,0:T(8,128)(2,1)S(1)}, u32[]{:S(2)}, u32[]{:S(2)}) async-start(bf16[4,2,32,1024]{3,2,1,0:T(8,128)(2,1)} %bitcast.120), calls=%async_computation.6 | async-start | bytes 1048576 | tf_op jit(solution)/shard_map/all_to_all | solution.py:94
  227.0 6.5 %all-to-all-done.6 = bf16[4,2,32,1024]{3,2,1,0:T(8,128)(2,1)S(1)} async-done(((bf16[4,2,32,1024]{3,2,1,0:T(8,128)(2,1)}), bf16[4,2,32,1024]{3,2,1,0:T(8,128)(2,1)S(1)}, u32[]{:S(2)}, u32[]{:S(2)}) %all-to-all-start.6) | async-done | bytes 524320 | tf_op jit(solution)/shard_map/all_to_all | solution.py:94
  242.8 3.5 %all-to-all-start.7 = ((bf16[4,2,32,1024]{3,2,1,0:T(8,128)(2,1)}), bf16[4,2,32,1024]{3,2,1,0:T(8,128)(2,1)S(1)}, u32[]{:S(2)}, u32[]{:S(2)}) async-start(bf16[4,2,32,1024]{3,2,1,0:T(8,128)(2,1)} %bitcast_dynamic-update-slice_fusion.8), calls=%async_computation.7 | async-start | bytes 1048576 | tf_op jit(solution)/shard_map/all_to_all | solution.py:147
  246.3 6.9 %multiply_subtract_fusion = f32[512,3584]{1,0:T(8,128)} fusion(bf16[512,3584]{1,0:T(8,128)(2,1)} %param.6, bf16[64,3584]{1,0:T(8,128)(2,1)} %collective-permute-done.14, bf16[64,3584]{1,0:T(8,128)(2,1)} %fusion.7, bf16[64,512]{1,0:T(8,128)(2,1)S(1)} %get-tuple-element.27, bf16[64,512]{1,0:T(8,128)(2,1)S(1)} %get-tuple-element.28), kind=kOutput, calls=%fused_computation | convolution fusion | flops 953417728 | bytes 12058624 | tf_op jit(solution)/shard_map/dot_general | solution.py:151
  (124 shorter events, 94.6 us)
Async XLA Ops:
  5.0 24.2 %all-to-all-start = ((f32[4,64,256]{2,1,0:T(8,128)}), f32[4,64,256]{2,1,0:T(8,128)S(1)}, u32[]{:S(2)}, u32[]{:S(2)}) async-start(f32[4,64,256]{2,1,0:T(8,128)} %broadcast_in_dim.80), calls=%async_computation | async-start | bytes 524288 | tf_op jit(solution)/shard_map/all_to_all | solution.py:31
  11.4 97.1 %collective-permute-start.4 = (bf16[128,3584]{1,0:T(8,128)(2,1)}, bf16[128,3584]{1,0:T(8,128)(2,1)}, u32[]{:S(2)}, u32[]{:S(2)}) collective-permute-start(bf16[128,3584]{1,0:T(8,128)(2,1)} %slice.95), channel_id=1, source_target_pairs={{0,4},{4,0},{8,12},{12,8},{16,20},{20,16},{24,28},{28,24},{1,5},{5... | collective-permute-start | bytes 2752520 | tf_op jit(solution)/shard_map/ppermute | solution.py:73
  16.4 55.8 %collective-permute-start.1 = (bf16[128,3584]{1,0:T(8,128)(2,1)}, bf16[128,3584]{1,0:T(8,128)(2,1)S(1)}, u32[]{:S(2)}, u32[]{:S(2)}) collective-permute-start(bf16[128,3584]{1,0:T(8,128)(2,1)} %get-tuple-element.37), channel_id=1, source_target_pairs={{0,24},{4,28},{8,0},{12,4},{16,8},{20,12},{24,16},{28,20},{1,25},{... | collective-permute-start | bytes 2752520 | tf_op jit(solution)/shard_map/ppermute | solution.py:130
  20.0 50.0 %collective-permute-start = (bf16[128,3584]{1,0:T(8,128)(2,1)}, bf16[128,3584]{1,0:T(8,128)(2,1)}, u32[]{:S(2)}, u32[]{:S(2)}) collective-permute-start(bf16[128,3584]{1,0:T(8,128)(2,1)} %get-tuple-element.38), channel_id=1, source_target_pairs={{0,8},{4,12},{8,16},{12,20},{16,24},{20,28},{24,0},{28,4},{1,9},{5... | collective-permute-start | bytes 2752520 | tf_op jit(solution)/shard_map/ppermute | solution.py:129
  30.2 35.1 %all-to-all-start.1 = ((f32[8,64,128]{2,1,0:T(8,128)}), f32[8,64,128]{2,1,0:T(8,128)S(1)}, u32[]{:S(2)}, u32[]{:S(2)}) async-start(f32[8,64,128]{2,1,0:T(8,128)} %bitcast_bitcast_fusion), calls=%async_computation.1 | async-start | bytes 524288 | tf_op jit(solution)/shard_map/all_to_all | solution.py:54
  66.1 12.2 %all-to-all-start.2 = ((f32[8,64,128]{2,1,0:T(8,128)}), f32[8,64,128]{2,1,0:T(8,128)S(1)}, u32[]{:S(2)}, u32[]{:S(2)}) async-start(f32[8,64,128]{2,1,0:T(8,128)} %broadcast_in_dim.81), calls=%async_computation.2 | async-start | bytes 524288 | tf_op jit(solution)/shard_map/all_to_all | solution.py:31
  79.8 10.9 %all-to-all-start.3 = ((f32[4,64,320]{2,1,0:T(8,128)}), f32[4,64,320]{2,1,0:T(8,128)S(1)}, u32[]{:S(2)}, u32[]{:S(2)}) async-start(f32[4,64,320]{2,1,0:T(8,128)} %broadcast_in_dim.82), calls=%async_computation.3 | async-start | bytes 786432 | tf_op jit(solution)/shard_map/all_to_all | solution.py:31
  85.5 47.2 %collective-permute-start.2 = (bf16[128,3584]{1,0:T(8,128)(2,1)}, bf16[128,3584]{1,0:T(8,128)(2,1)}, u32[]{:S(2)}, u32[]{:S(2)}) collective-permute-start(bf16[128,3584]{1,0:T(8,128)(2,1)} %collective-permute-done), channel_id=1, source_target_pairs={{0,8},{4,12},{8,16},{12,20},{16,24},{20,28},{24,0},{28,4},{1,9},{5... | collective-permute-start | bytes 2752520 | tf_op jit(solution)/shard_map/ppermute | solution.py:129
  85.6 47.0 %collective-permute-start.3 = (bf16[128,3584]{1,0:T(8,128)(2,1)S(1)}, bf16[128,3584]{1,0:T(8,128)(2,1)}, u32[]{:S(2)}, u32[]{:S(2)}) collective-permute-start(bf16[128,3584]{1,0:T(8,128)(2,1)S(1)} %collective-permute-done.1), channel_id=1, source_target_pairs={{0,24},{4,28},{8,0},{12,4},{16,8},{20,12},{24,16},{28,20},{1,25},{... | collective-permute-start | bytes 2752520 | tf_op jit(solution)/shard_map/ppermute | solution.py:130
  89.3 61.8 %collective-permute-start.7 = (bf16[384,3584]{1,0:T(8,128)(2,1)}, bf16[384,3584]{1,0:T(8,128)(2,1)}, u32[]{:S(2)}, u32[]{:S(2)}) collective-permute-start(bf16[384,3584]{1,0:T(8,128)(2,1)} %slice.88), channel_id=1, source_target_pairs={{0,4},{4,0},{8,12},{12,8},{16,20},{20,16},{24,28},{28,24},{1,5},{5... | collective-permute-start | bytes 8257544 | tf_op jit(solution)/shard_map/ppermute | solution.py:124
  104.1 28.5 %all-to-all-start.4 = ((f32[4,64,256]{2,1,0:T(8,128)}), f32[4,64,256]{2,1,0:T(8,128)S(1)}, u32[]{:S(2)}, u32[]{:S(2)}) async-start(f32[4,64,256]{2,1,0:T(8,128)} %broadcast_in_dim.83), calls=%async_computation.4 | async-start | bytes 524288 | tf_op jit(solution)/shard_map/all_to_all | solution.py:31
  132.7 72.9 %collective-permute-start.5 = (bf16[128,3584]{1,0:T(8,128)(2,1)}, bf16[128,3584]{1,0:T(8,128)(2,1)S(1)}, u32[]{:S(2)}, u32[]{:S(2)}) collective-permute-start(bf16[128,3584]{1,0:T(8,128)(2,1)} %collective-permute-done.2), channel_id=1, source_target_pairs={{0,8},{4,12},{8,16},{12,20},{16,24},{20,28},{24,0},{28,4},{1,9},{5... | collective-permute-start | bytes 2752520 | tf_op jit(solution)/shard_map/ppermute | solution.py:129
  134.8 70.8 %collective-permute-start.6 = (bf16[128,3584]{1,0:T(8,128)(2,1)}, bf16[128,3584]{1,0:T(8,128)(2,1)}, u32[]{:S(2)}, u32[]{:S(2)}) collective-permute-start(bf16[128,3584]{1,0:T(8,128)(2,1)} %collective-permute-done.3), channel_id=1, source_target_pairs={{0,24},{4,28},{8,0},{12,4},{16,8},{20,12},{24,16},{28,20},{1,25},{... | collective-permute-start | bytes 2752520 | tf_op jit(solution)/shard_map/ppermute | solution.py:130
  162.8 23.6 %all-to-all-start.5 = ((bf16[4,6,32,1024]{3,2,1,0:T(8,128)(2,1)}), bf16[4,6,32,1024]{3,2,1,0:T(8,128)(2,1)S(1)}, u32[]{:S(2)}, u32[]{:S(2)}) async-start(bf16[4,6,32,1024]{3,2,1,0:T(8,128)(2,1)} %copy.30), calls=%async_computation.5 | async-start | bytes 3145728 | tf_op jit(solution)/shard_map/all_to_all | solution.py:94
  187.3 33.9 %all-to-all-start.8 = ((f32[4,64,512]{2,1,0:T(8,128)}), f32[4,64,512]{2,1,0:T(8,128)S(1)}, u32[]{:S(2)}, u32[]{:S(2)}) async-start(f32[4,64,512]{2,1,0:T(8,128)} %broadcast_in_dim.100), calls=%async_computation.8 | async-start | bytes 1048576 | tf_op jit(solution)/shard_map/all_to_all | solution.py:31
  192.6 4.5 %collective-permute-start.8 = (bf16[32,1024]{1,0:T(8,128)(2,1)S(1)}, bf16[32,1024]{1,0:T(8,128)(2,1)S(1)}, u32[]{:S(2)}, u32[]{:S(2)}) collective-permute-start(bf16[32,1024]{1,0:T(8,128)(2,1)S(1)} %get-tuple-element.46), channel_id=1, source_target_pairs={{0,24},{4,28},{8,0},{12,4},{16,8},{20,12},{24,16},{28,20},{1,25},{... | collective-permute-start | bytes 196616 | tf_op jit(solution)/shard_map/ppermute | solution.py:102
  193.5 11.4 %collective-permute-start.11 = (bf16[32,1024]{1,0:T(8,128)(2,1)S(1)}, bf16[32,1024]{1,0:T(8,128)(2,1)S(1)}, u32[]{:S(2)}, u32[]{:S(2)}) collective-permute-start(bf16[32,1024]{1,0:T(8,128)(2,1)S(1)} %get-tuple-element.43), channel_id=1, source_target_pairs={{0,16},{4,20},{8,24},{12,28},{16,0},{20,4},{24,8},{28,12},{1,17},{... | collective-permute-start | bytes 196616 | tf_op jit(solution)/shard_map/ppermute | solution.py:102
  193.5 10.7 %collective-permute-start.10 = (bf16[32,1024]{1,0:T(8,128)(2,1)S(1)}, bf16[32,1024]{1,0:T(8,128)(2,1)S(1)}, u32[]{:S(2)}, u32[]{:S(2)}) collective-permute-start(bf16[32,1024]{1,0:T(8,128)(2,1)S(1)} %get-tuple-element.44), channel_id=1, source_target_pairs={{0,16},{4,20},{8,24},{12,28},{16,0},{20,4},{24,8},{28,12},{1,17},{... | collective-permute-start | bytes 196616 | tf_op jit(solution)/shard_map/ppermute | solution.py:102
  197.1 6.1 %collective-permute-start.9 = (bf16[32,1024]{1,0:T(8,128)(2,1)S(1)}, bf16[32,1024]{1,0:T(8,128)(2,1)S(1)}, u32[]{:S(2)}, u32[]{:S(2)}) collective-permute-start(bf16[32,1024]{1,0:T(8,128)(2,1)S(1)} %get-tuple-element.45), channel_id=1, source_target_pairs={{0,8},{4,12},{8,16},{12,20},{16,24},{20,28},{24,0},{28,4},{1,9},{5... | collective-permute-start | bytes 196616 | tf_op jit(solution)/shard_map/ppermute | solution.py:102
  221.2 12.3 %all-to-all-start.6 = ((bf16[4,2,32,1024]{3,2,1,0:T(8,128)(2,1)}), bf16[4,2,32,1024]{3,2,1,0:T(8,128)(2,1)S(1)}, u32[]{:S(2)}, u32[]{:S(2)}) async-start(bf16[4,2,32,1024]{3,2,1,0:T(8,128)(2,1)} %bitcast.120), calls=%async_computation.6 | async-start | bytes 1048576 | tf_op jit(solution)/shard_map/all_to_all | solution.py:94
  225.5 13.2 %collective-permute-start.14 = (bf16[64,3584]{1,0:T(8,128)(2,1)}, bf16[64,3584]{1,0:T(8,128)(2,1)}, u32[]{:S(2)}, u32[]{:S(2)}) collective-permute-start(bf16[64,3584]{1,0:T(8,128)(2,1)} %fusion.7), channel_id=1, source_target_pairs={{0,4},{4,0},{8,12},{12,8},{16,20},{20,16},{24,28},{28,24},{1,5},{5... | collective-permute-start | bytes 1376264 | tf_op jit(solution)/shard_map/ppermute | solution.py:140
  233.6 8.6 %collective-permute-start.13 = (bf16[32,1024]{1,0:T(8,128)(2,1)S(1)}, bf16[32,1024]{1,0:T(8,128)(2,1)S(1)}, u32[]{:S(2)}, u32[]{:S(2)}) collective-permute-start(bf16[32,1024]{1,0:T(8,128)(2,1)S(1)} %get-tuple-element.47), channel_id=1, source_target_pairs={{0,24},{4,28},{8,0},{12,4},{16,8},{20,12},{24,16},{28,20},{1,25},{... | collective-permute-start | bytes 196616 | tf_op jit(solution)/shard_map/ppermute | solution.py:102
  235.5 6.1 %collective-permute-start.12 = (bf16[32,1024]{1,0:T(8,128)(2,1)S(1)}, bf16[32,1024]{1,0:T(8,128)(2,1)S(1)}, u32[]{:S(2)}, u32[]{:S(2)}) collective-permute-start(bf16[32,1024]{1,0:T(8,128)(2,1)S(1)} %get-tuple-element.48), channel_id=1, source_target_pairs={{0,8},{4,12},{8,16},{12,20},{16,24},{20,28},{24,0},{28,4},{1,9},{5... | collective-permute-start | bytes 196616 | tf_op jit(solution)/shard_map/ppermute | solution.py:102
  242.8 12.3 %all-to-all-start.7 = ((bf16[4,2,32,1024]{3,2,1,0:T(8,128)(2,1)}), bf16[4,2,32,1024]{3,2,1,0:T(8,128)(2,1)S(1)}, u32[]{:S(2)}, u32[]{:S(2)}) async-start(bf16[4,2,32,1024]{3,2,1,0:T(8,128)(2,1)} %bitcast_dynamic-update-slice_fusion.8), calls=%async_computation.7 | async-start | bytes 1048576 | tf_op jit(solution)/shard_map/all_to_all | solution.py:147
  (9 other events, 120.7 us)

commit v6 on v4

--- a/solution.py
+++ b/solution.py
@@ -68,24 +68,23 @@
         basis_mine = jnp.dot(inverse, rows, precision=highest)
         return token_proj, basis_mine
 
-    cut = row_count // 2
-    others = [lax.ppermute(weight[:cut], "dp", swap)]
+    left = left_stage()
+    weight_sent, upper, under, left = tie((weight, grad_output[:half], grad_output[half:], left))
+    own, other = weight, lax.ppermute(weight_sent, "dp", swap)
     low = index % 2 == 0
     columns = 2 * row_count
     piece_rows = half // width
-    upper, under = grad_output[:half], grad_output[half:]
     gathered = jnp.zeros((groups, 2, half, grad_output.shape[1]), jnp.bfloat16)
     returned = jnp.zeros((groups, 2, piece_rows, columns), jnp.bfloat16)
 
     def reduced(pieces):
         rows = jnp.concatenate(pieces, axis=0)
-        mine, *rest = (
+        mine, rest = (
             lax.dot_general(
                 rows, part, (((1,), (1,)), ((), ())), preferred_element_type=jnp.float32
             ).astype(jnp.bfloat16)
-            for part in (weight, *others)
+            for part in (own, other)
         )
-        rest = jnp.concatenate(rest, axis=1)
         product = jnp.concatenate(
             [jnp.where(low, mine, rest), jnp.where(low, rest, mine)], axis=1
         )
@@ -117,15 +116,13 @@
             pieces.append(piece)
         if step + 1 < groups:
             if step == 1:
-                left = left_stage()
-                weight_sent, upper, under, left = tie((weight[cut:], upper, under, left))
-                others.append(lax.ppermute(weight_sent, "dp", swap))
+                upper, under, token_proj = tie((upper, under, token_proj))
             if step == groups - 2:
-                upper, under, others[1], token_proj = tie((upper, under, others[1], token_proj))
+                upper, under, own, other = tie((upper, under, own, other))
             upper = lax.ppermute(upper, "dp", ahead)
             under = lax.ppermute(under, "dp", behind)
-            if step == 1:
-                token_proj, basis_mine = basis_stage(left)
+        if step == 0:
+            token_proj, basis_mine = basis_stage(left)
     token_proj = spread(token_proj, "dp", along)
 
     rank = start_basis.shape[1]

time: 256 us -> 256 us (level)
  waiting for transfers between devices: 91.6 us -> 66.9 us
  blocking collectives: 0 us -> 14.9 us
  other arithmetic: 16.9 us -> 28.1 us
  starting transfers between devices: 58.4 us -> 54 us
  local copies, waits for them, and re-layouts: 52.4 us -> 56.2 us
    all_to_all x1 -> x0, waiting for transfers between devices: 29.5 us -> none  [left_stage(): left_piece = lax.all_to_all(pieces, 'dp', 0, 0, tiled=True).sum(0)]
    all_to_all x0 -> x1, blocking collectives: none -> 14.9 us  [left_stage(): left_piece = lax.all_to_all(pieces, 'dp', 0, 0, tiled=True).sum(0)]
    all_to_all x5, waiting for transfers between devices: 34.3 us -> 41.8 us  [spread(): lax.all_to_all(copies, axis, 0, 0, axis_index_groups=groups, tiled=True)]
    dot_general x6 -> x4, matrix products: 20.3 us -> 14.2 us  [reduced(): lax.dot_general(rows, part, (((1,), (1,)), ((), ())), preferred_element_t...]
    unnamed x22 -> x27, local copies, waits for them, and re-layouts: 8.4 us -> 14.4 us
    slice x2 -> x1, local copies, waits for them, and re-layouts: 7.18 us -> 2.5 us  [body(): grad_output[half:]]
    all_to_all x1 -> x0, starting transfers between devices: 3.41 us -> none  [left_stage(): left_piece = lax.all_to_all(pieces, 'dp', 0, 0, tiled=True).sum(0)]
    all_to_all x2, waiting for transfers between devices: 2.85 us -> 0.01 us  [reduced(): parts = lax.all_to_all(product, 'tensor', 0, 0, tiled=True)]
  transfers between devices with their start and end apart: 24 -> 22, of which waited for: 12 -> 9; matrix products, arithmetic and copies ran while one was open for 38% -> 42% of each run, Pallas kernels for 0% -> 0%
where the time goes in v6:
time: 256 us; the launch traced here: 254 us
  waiting for transfers between devices  66.9 us (26%)
  local copies, waits for them, and re-layouts  56.2 us (22%)
  starting transfers between devices  54 us (21%)
  matrix products  32.4 us (13%)
  other arithmetic  28.1 us (11%)
  blocking collectives  14.9 us (6%)
    all_to_all x5, waiting for transfers between devices, spread(): lax.all_to_all(copies, axis, 0, 0, axis_index_groups=groups, tiled=True)  41.8 us
    all_to_all x5, starting transfers between devices, spread(): lax.all_to_all(copies, axis, 0, 0, axis_index_groups=groups, tiled=True)  18.8 us
    ppermute x3, waiting for transfers between devices, body(): under = lax.ppermute(under, 'dp', behind)  17.1 us
    all_to_all x1, blocking collectives, left_stage(): left_piece = lax.all_to_all(pieces, 'dp', 0, 0, tiled=True).sum(0)  14.9 us
    unnamed x27, local copies, waits for them, and re-layouts  14.4 us
    dot_general x4, matrix products, reduced(): lax.dot_general(rows, part, (((1,), (1,)), ((), ())), preferred_element_t...  14.2 us
    dynamic_update_slice x8, local copies, waits for them, and re-layouts, body(): lax.dynamic_update_slice(gathered, piece[None, None], (source, place, 0, 0))  13.7 us
    ppermute x6, starting transfers between devices, give_back(): value = lax.ppermute(value, 'dp', back)  9.08 us
  transfers between devices with their start and end apart: 22, of which 9 were waited for; matrix products, arithmetic and copies ran while one was open for 42% of the time, Pallas kernels for 0%

profile of v6, /device:TPU:0, one launch (start us, length us, event | category | flops | bytes accessed | tf_op | source)
XLA Modules:
  0.0 253.6 jit_solution(18188383973728841305)
XLA Ops:
  5.0 4.2 %all-to-all-start = ((f32[4,64,256]{2,1,0:T(8,128)}), f32[4,64,256]{2,1,0:T(8,128)S(1)}, u32[]{:S(2)}, u32[]{:S(2)}) async-start(f32[4,64,256]{2,1,0:T(8,128)} %broadcast_in_dim.81), calls=%async_computation | async-start | bytes 524288 | tf_op jit(solution)/shard_map/all_to_all | solution.py:31
  9.2 6.0 %all-to-all-done = f32[4,64,256]{2,1,0:T(8,128)S(1)} async-done(((f32[4,64,256]{2,1,0:T(8,128)}), f32[4,64,256]{2,1,0:T(8,128)S(1)}, u32[]{:S(2)}, u32[]{:S(2)}) %all-to-all-start) | async-done | bytes 262176 | tf_op jit(solution)/shard_map/all_to_all | solution.py:31
  15.6 14.9 %all_to_all.45 = f32[8,64,128]{2,1,0:T(8,128)S(1)} all-to-all(f32[8,64,128]{2,1,0:T(8,128)S(1)} %bitcast_bitcast_fusion), channel_id=1, replica_groups=mesh['dp'=8,'tensor'=4] {'dp'}, dimensions={0} | all-to-all | bytes 524288 | tf_op jit(solution)/shard_map/all_to_all | solution.py:54
  31.3 3.6 %all-to-all-start.2 = ((f32[8,64,128]{2,1,0:T(8,128)}), f32[8,64,128]{2,1,0:T(8,128)S(1)}, u32[]{:S(2)}, u32[]{:S(2)}) async-start(f32[8,64,128]{2,1,0:T(8,128)} %broadcast_in_dim.82), calls=%async_computation.2 | async-start | bytes 524288 | tf_op jit(solution)/shard_map/all_to_all | solution.py:31
  37.4 6.1 %all-to-all-done.2 = f32[8,64,128]{2,1,0:T(8,128)S(1)} async-done(((f32[8,64,128]{2,1,0:T(8,128)}), f32[8,64,128]{2,1,0:T(8,128)S(1)}, u32[]{:S(2)}, u32[]{:S(2)}) %all-to-all-start.2) | async-done | bytes 262176 | tf_op jit(solution)/shard_map/all_to_all | solution.py:31
  52.3 4.1 %all-to-all-start.3 = ((f32[4,64,320]{2,1,0:T(8,128)}), f32[4,64,320]{2,1,0:T(8,128)}, u32[]{:S(2)}, u32[]{:S(2)}) async-start(f32[4,64,320]{2,1,0:T(8,128)} %broadcast_in_dim.83), calls=%async_computation.3 | async-start | bytes 786432 | tf_op jit(solution)/shard_map/all_to_all | solution.py:31
  57.9 3.7 %broadcast_in_dim.91 = bf16[4,2,128,3584]{3,2,1,0:T(8,128)(2,1)} broadcast(bf16[]{:T(256)} %constant.160.clone.1), dimensions={} | broadcast | bytes 7340034 | tf_op jit(solution)/shard_map/broadcast_in_dim | solution.py:77
  64.7 3.5 %all-to-all-start.8 = ((f32[4,64,512]{2,1,0:T(8,128)}), f32[4,64,512]{2,1,0:T(8,128)S(1)}, u32[]{:S(2)}, u32[]{:S(2)}) async-start(f32[4,64,512]{2,1,0:T(8,128)} %broadcast_in_dim.100), calls=%async_computation.8 | async-start | bytes 1048576 | tf_op jit(solution)/shard_map/all_to_all | solution.py:31
  74.1 7.2 %cholesky.17 = f32[64,64]{1,0:T(8,128)} custom-call(f32[64,64]{1,0:T(8,128)} %fusion.45), custom_call_target="Cholesky" | custom-call | tf_op jit(solution)/shard_map/jit(cholesky)/cholesky | solution.py:62
  84.7 6.3 %custom-call.7 = f32[1,64,64]{1,2,0:T(8,128)} custom-call(f32[1,64,64]{2,1,0:T(8,128)} %fusion.42), custom_call_target="InvertDiagBlocksLowerTriangular" | custom-call | tf_op jit(solution)/shard_map/jit(_solve_triangular)/triangular_solve | solution.py:63
  96.0 3.8 %collective-permute-start.3 = (bf16[128,3584]{1,0:T(8,128)(2,1)}, bf16[128,3584]{1,0:T(8,128)(2,1)S(1)}, u32[]{:S(2)}, u32[]{:S(2)}) collective-permute-start(bf16[128,3584]{1,0:T(8,128)(2,1)} %collective-permute-done.1), channel_id=1, source_target_pairs={{0,24},{4,28},{8,0},{12,4},{16,8},{20,12},{24,16},{28,20},{1,25},{... | collective-permute-start | bytes 2752520 | tf_op jit(solution)/shard_map/ppermute | solution.py:123
  101.3 3.4 %all-to-all-start.7 = ((f32[4,64,256]{2,1,0:T(8,128)}), f32[4,64,256]{2,1,0:T(8,128)S(1)}, u32[]{:S(2)}, u32[]{:S(2)}) async-start(f32[4,64,256]{2,1,0:T(8,128)} %broadcast_in_dim.90), calls=%async_computation.7 | async-start | bytes 524288 | tf_op jit(solution)/shard_map/all_to_all | solution.py:31
  113.4 29.4 %all-to-all-done.7 = f32[4,64,256]{2,1,0:T(8,128)S(1)} async-done(((f32[4,64,256]{2,1,0:T(8,128)}), f32[4,64,256]{2,1,0:T(8,128)S(1)}, u32[]{:S(2)}, u32[]{:S(2)}) %all-to-all-start.7) | async-done | bytes 262176 | tf_op jit(solution)/shard_map/all_to_all | solution.py:31
  153.1 6.7 %convolution_convert_fusion = bf16[768,512]{0,1:T(8,128)(2,1)S(1)} fusion(bf16[768,3584]{1,0:T(8,128)(2,1)} %constant_dynamic-update-slice_fusion, bf16[512,3584]{1,0:T(8,128)(2,1)} %collective-permute-done.4), kind=kOutput, calls=%fused_computation.9 | convolution fusion | flops 2818965504 | bytes 9961472 | tf_op jit(solution)/shard_map/dot_general | solution.py:83
  159.8 3.0 %broadcast_select_fusion.1 = (bf16[768,512]{0,1:T(8,128)(2,1)S(1)}, bf16[768,512]{0,1:T(8,128)(2,1)S(1)}) fusion(bf16[768,512]{0,1:T(8,128)(2,1)S(1)} %convolution_convert_fusion, pred[]{:T(512)S(6)} %eq.23, bf16[768,3584]{1,0:T(8,128)(2,1)S(1)} %bitcast.124, bf16[512,3584]{1,0:T(8,128)(2,1)S(1)} %copy-done.6), kind=kOutput, calls=%fused_computation.32 | convolution fusion | flops 2819751936 | bytes 11534337 | tf_op jit(solution)/shard_map/dot_general | solution.py:83
  169.5 4.5 %all-to-all-start.4 = ((bf16[4,6,32,1024]{3,2,1,0:T(8,128)(2,1)}), bf16[4,6,32,1024]{3,2,1,0:T(8,128)(2,1)}, u32[]{:S(2)}, u32[]{:S(2)}) async-start(bf16[4,6,32,1024]{3,2,1,0:T(8,128)(2,1)} %copy.26), calls=%async_computation.4 | async-start | bytes 3145728 | tf_op jit(solution)/shard_map/all_to_all | solution.py:92
  175.9 17.1 %collective-permute-done.10 = bf16[128,3584]{1,0:T(8,128)(2,1)} collective-permute-done((bf16[128,3584]{1,0:T(8,128)(2,1)S(1)}, bf16[128,3584]{1,0:T(8,128)(2,1)}, u32[]{:S(2)}, u32[]{:S(2)}) %collective-permute-start.10) | collective-permute-done | bytes 917536 | tf_op jit(solution)/shard_map/ppermute | solution.py:123
  194.3 3.3 %convolution_convert_fusion.2 = bf16[256,512]{1,0:T(8,128)(2,1)S(1)} fusion(bf16[256,3584]{1,0:T(8,128)(2,1)S(1)} %constant_dynamic-update-slice_fusion.6, bf16[512,3584]{1,0:T(8,128)(2,1)} %collective-permute-done.4), kind=kOutput, calls=%fused_computation.11 | convolution fusion | flops 939655168 | bytes 5767168 | tf_op jit(solution)/shard_map/dot_general | solution.py:83
  204.0 4.2 %fusion.21 = f32[128,3584]{1,0:T(8,128)S(1)} fusion(bf16[1024,3584]{1,0:T(8,128)(2,1)} %bitcast.39, bf16[64,1024]{1,0:T(8,128)(2,1)S(1)} %get-tuple-element.27, bf16[64,1024]{1,0:T(8,128)(2,1)S(1)} %get-tuple-element.28), kind=kOutput, calls=%fused_computation.46 | convolution fusion | flops 940048384 | bytes 9437184 | tf_op jit(solution)/shard_map/dot_general | solution.py:19
  211.7 3.5 %all-to-all-start.5 = ((bf16[4,2,32,1024]{3,2,1,0:T(8,128)(2,1)}), bf16[4,2,32,1024]{3,2,1,0:T(8,128)(2,1)S(1)}, u32[]{:S(2)}, u32[]{:S(2)}) async-start(bf16[4,2,32,1024]{3,2,1,0:T(8,128)(2,1)} %bitcast.116), calls=%async_computation.5 | async-start | bytes 1048576 | tf_op jit(solution)/shard_map/all_to_all | solution.py:92
  225.6 3.2 %collective-permute-done.6 = bf16[32,1024]{1,0:T(8,128)(2,1)S(1)} collective-permute-done((bf16[32,1024]{1,0:T(8,128)(2,1)S(1)}, bf16[32,1024]{1,0:T(8,128)(2,1)S(1)}, u32[]{:S(2)}, u32[]{:S(2)}) %collective-permute-start.6) | collective-permute-done | bytes 65568 | tf_op jit(solution)/shard_map/ppermute | solution.py:100
  233.5 3.8 %collective-permute-start.12 = (bf16[32,1024]{1,0:T(8,128)(2,1)S(1)}, bf16[32,1024]{1,0:T(8,128)(2,1)S(1)}, u32[]{:S(2)}, u32[]{:S(2)}) collective-permute-start(bf16[32,1024]{1,0:T(8,128)(2,1)S(1)} %get-tuple-element.45), channel_id=1, source_target_pairs={{0,24},{4,28},{8,0},{12,4},{16,8},{20,12},{24,16},{28,20},{1,25},{... | collective-permute-start | bytes 196616 | tf_op jit(solution)/shard_map/ppermute | solution.py:100
  240.2 3.5 %all-to-all-start.6 = ((bf16[4,2,32,1024]{3,2,1,0:T(8,128)(2,1)}), bf16[4,2,32,1024]{3,2,1,0:T(8,128)(2,1)S(1)}, u32[]{:S(2)}, u32[]{:S(2)}) async-start(bf16[4,2,32,1024]{3,2,1,0:T(8,128)(2,1)} %bitcast_dynamic-update-slice_fusion.8), calls=%async_computation.6 | async-start | bytes 1048576 | tf_op jit(solution)/shard_map/all_to_all | solution.py:141
  246.2 6.6 %multiply_subtract_fusion = f32[512,3584]{1,0:T(8,128)} fusion(bf16[512,3584]{1,0:T(8,128)(2,1)} %param.6, bf16[64,3584]{1,0:T(8,128)(2,1)S(1)} %collective-permute-done.13, bf16[64,3584]{1,0:T(8,128)(2,1)} %fusion.7, bf16[64,512]{1,0:T(8,128)(2,1)S(1)} %copy-done.5, bf16[64,512]{1,0:T(8,128)(2,1)} %get-tuple-element.26), kind=kOutput, calls=%fused_computation | convolution fusion | flops 953417728 | bytes 12058624 | tf_op jit(solution)/shard_map/dot_general | solution.py:145
  (121 shorter events, 96.9 us)
Async XLA Ops:
  0.6 14.7 %copy-start = (bf16[256,4096]{1,0:T(8,128)(2,1)S(1)}, bf16[256,4096]{1,0:T(8,128)(2,1)}, u32[]{:S(2)}) copy-start(bf16[256,4096]{1,0:T(8,128)(2,1)} %param.4) | copy-start | bytes 6291460
  5.0 10.3 %all-to-all-start = ((f32[4,64,256]{2,1,0:T(8,128)}), f32[4,64,256]{2,1,0:T(8,128)S(1)}, u32[]{:S(2)}, u32[]{:S(2)}) async-start(f32[4,64,256]{2,1,0:T(8,128)} %broadcast_in_dim.81), calls=%async_computation | async-start | bytes 524288 | tf_op jit(solution)/shard_map/all_to_all | solution.py:31
  31.3 12.2 %all-to-all-start.2 = ((f32[8,64,128]{2,1,0:T(8,128)}), f32[8,64,128]{2,1,0:T(8,128)S(1)}, u32[]{:S(2)}, u32[]{:S(2)}) async-start(f32[8,64,128]{2,1,0:T(8,128)} %broadcast_in_dim.82), calls=%async_computation.2 | async-start | bytes 524288 | tf_op jit(solution)/shard_map/all_to_all | solution.py:31
  44.7 51.2 %collective-permute-start = (bf16[128,3584]{1,0:T(8,128)(2,1)}, bf16[128,3584]{1,0:T(8,128)(2,1)}, u32[]{:S(2)}, u32[]{:S(2)}) collective-permute-start(bf16[128,3584]{1,0:T(8,128)(2,1)} %get-tuple-element.14), channel_id=1, source_target_pairs={{0,8},{4,12},{8,16},{12,20},{16,24},{20,28},{24,0},{28,4},{1,9},{5... | collective-permute-start | bytes 2752520 | tf_op jit(solution)/shard_map/ppermute | solution.py:122
  46.3 49.7 %collective-permute-start.1 = (bf16[128,3584]{1,0:T(8,128)(2,1)S(1)}, bf16[128,3584]{1,0:T(8,128)(2,1)}, u32[]{:S(2)}, u32[]{:S(2)}) collective-permute-start(bf16[128,3584]{1,0:T(8,128)(2,1)S(1)} %get-tuple-element.15), channel_id=1, source_target_pairs={{0,24},{4,28},{8,0},{12,4},{16,8},{20,12},{24,16},{28,20},{1,25},{... | collective-permute-start | bytes 2752520 | tf_op jit(solution)/shard_map/ppermute | solution.py:123
  52.3 11.6 %all-to-all-start.3 = ((f32[4,64,320]{2,1,0:T(8,128)}), f32[4,64,320]{2,1,0:T(8,128)}, u32[]{:S(2)}, u32[]{:S(2)}) async-start(f32[4,64,320]{2,1,0:T(8,128)} %broadcast_in_dim.83), calls=%async_computation.3 | async-start | bytes 786432 | tf_op jit(solution)/shard_map/all_to_all | solution.py:31
  56.4 92.9 %collective-permute-start.4 = (bf16[512,3584]{1,0:T(8,128)(2,1)}, bf16[512,3584]{1,0:T(8,128)(2,1)}, u32[]{:S(2)}, u32[]{:S(2)}) collective-permute-start(bf16[512,3584]{1,0:T(8,128)(2,1)} %param.6), channel_id=1, source_target_pairs={{0,4},{4,0},{8,12},{12,8},{16,20},{20,16},{24,28},{28,24},{1,5},{5... | collective-permute-start | bytes 11010056 | tf_op jit(solution)/shard_map/ppermute | solution.py:73
  64.7 29.5 %all-to-all-start.8 = ((f32[4,64,512]{2,1,0:T(8,128)}), f32[4,64,512]{2,1,0:T(8,128)S(1)}, u32[]{:S(2)}, u32[]{:S(2)}) async-start(f32[4,64,512]{2,1,0:T(8,128)} %broadcast_in_dim.100), calls=%async_computation.8 | async-start | bytes 1048576 | tf_op jit(solution)/shard_map/all_to_all | solution.py:31
  95.9 47.0 %collective-permute-start.2 = (bf16[128,3584]{1,0:T(8,128)(2,1)}, bf16[128,3584]{1,0:T(8,128)(2,1)}, u32[]{:S(2)}, u32[]{:S(2)}) collective-permute-start(bf16[128,3584]{1,0:T(8,128)(2,1)} %collective-permute-done), channel_id=1, source_target_pairs={{0,8},{4,12},{8,16},{12,20},{16,24},{20,28},{24,0},{28,4},{1,9},{5... | collective-permute-start | bytes 2752520 | tf_op jit(solution)/shard_map/ppermute | solution.py:122
  96.0 49.1 %collective-permute-start.3 = (bf16[128,3584]{1,0:T(8,128)(2,1)}, bf16[128,3584]{1,0:T(8,128)(2,1)S(1)}, u32[]{:S(2)}, u32[]{:S(2)}) collective-permute-start(bf16[128,3584]{1,0:T(8,128)(2,1)} %collective-permute-done.1), channel_id=1, source_target_pairs={{0,24},{4,28},{8,0},{12,4},{16,8},{20,12},{24,16},{28,20},{1,25},{... | collective-permute-start | bytes 2752520 | tf_op jit(solution)/shard_map/ppermute | solution.py:123
  101.3 41.5 %all-to-all-start.7 = ((f32[4,64,256]{2,1,0:T(8,128)}), f32[4,64,256]{2,1,0:T(8,128)S(1)}, u32[]{:S(2)}, u32[]{:S(2)}) async-start(f32[4,64,256]{2,1,0:T(8,128)} %broadcast_in_dim.90), calls=%async_computation.7 | async-start | bytes 524288 | tf_op jit(solution)/shard_map/all_to_all | solution.py:31
  149.2 25.4 %collective-permute-start.9 = (bf16[128,3584]{1,0:T(8,128)(2,1)}, bf16[128,3584]{1,0:T(8,128)(2,1)}, u32[]{:S(2)}, u32[]{:S(2)}) collective-permute-start(bf16[128,3584]{1,0:T(8,128)(2,1)} %collective-permute-done.2), channel_id=1, source_target_pairs={{0,8},{4,12},{8,16},{12,20},{16,24},{20,28},{24,0},{28,4},{1,9},{5... | collective-permute-start | bytes 2752520 | tf_op jit(solution)/shard_map/ppermute | solution.py:122
  151.6 41.4 %collective-permute-start.10 = (bf16[128,3584]{1,0:T(8,128)(2,1)S(1)}, bf16[128,3584]{1,0:T(8,128)(2,1)}, u32[]{:S(2)}, u32[]{:S(2)}) collective-permute-start(bf16[128,3584]{1,0:T(8,128)(2,1)S(1)} %collective-permute-done.3), channel_id=1, source_target_pairs={{0,24},{4,28},{8,0},{12,4},{16,8},{20,12},{24,16},{28,20},{1,25},{... | collective-permute-start | bytes 2752520 | tf_op jit(solution)/shard_map/ppermute | solution.py:123
  169.5 42.2 %all-to-all-start.4 = ((bf16[4,6,32,1024]{3,2,1,0:T(8,128)(2,1)}), bf16[4,6,32,1024]{3,2,1,0:T(8,128)(2,1)}, u32[]{:S(2)}, u32[]{:S(2)}) async-start(bf16[4,6,32,1024]{3,2,1,0:T(8,128)(2,1)} %copy.26), calls=%async_computation.4 | async-start | bytes 3145728 | tf_op jit(solution)/shard_map/all_to_all | solution.py:92
  210.3 33.4 %collective-permute-start.13 = (bf16[64,3584]{1,0:T(8,128)(2,1)}, bf16[64,3584]{1,0:T(8,128)(2,1)S(1)}, u32[]{:S(2)}, u32[]{:S(2)}) collective-permute-start(bf16[64,3584]{1,0:T(8,128)(2,1)} %fusion.7), channel_id=1, source_target_pairs={{0,4},{4,0},{8,12},{12,8},{16,20},{20,16},{24,28},{28,24},{1,5},{5... | collective-permute-start | bytes 1376264 | tf_op jit(solution)/shard_map/ppermute | solution.py:134
  211.7 20.9 %all-to-all-start.5 = ((bf16[4,2,32,1024]{3,2,1,0:T(8,128)(2,1)}), bf16[4,2,32,1024]{3,2,1,0:T(8,128)(2,1)S(1)}, u32[]{:S(2)}, u32[]{:S(2)}) async-start(bf16[4,2,32,1024]{3,2,1,0:T(8,128)(2,1)} %bitcast.116), calls=%async_computation.5 | async-start | bytes 1048576 | tf_op jit(solution)/shard_map/all_to_all | solution.py:92
  217.0 29.2 %copy-start.5 = (bf16[64,512]{1,0:T(8,128)(2,1)S(1)}, bf16[64,512]{1,0:T(8,128)(2,1)}, u32[]{:S(2)}) copy-start(bf16[64,512]{1,0:T(8,128)(2,1)} %get-tuple-element.25) | copy-start | bytes 196612
  219.1 5.9 %collective-permute-start.5 = (bf16[32,1024]{1,0:T(8,128)(2,1)S(1)}, bf16[32,1024]{1,0:T(8,128)(2,1)S(1)}, u32[]{:S(2)}, u32[]{:S(2)}) collective-permute-start(bf16[32,1024]{1,0:T(8,128)(2,1)S(1)} %get-tuple-element.44), channel_id=1, source_target_pairs={{0,24},{4,28},{8,0},{12,4},{16,8},{20,12},{24,16},{28,20},{1,25},{... | collective-permute-start | bytes 196616 | tf_op jit(solution)/shard_map/ppermute | solution.py:100
  222.0 6.8 %collective-permute-start.6 = (bf16[32,1024]{1,0:T(8,128)(2,1)S(1)}, bf16[32,1024]{1,0:T(8,128)(2,1)S(1)}, u32[]{:S(2)}, u32[]{:S(2)}) collective-permute-start(bf16[32,1024]{1,0:T(8,128)(2,1)S(1)} %get-tuple-element.43), channel_id=1, source_target_pairs={{0,8},{4,12},{8,16},{12,20},{16,24},{20,28},{24,0},{28,4},{1,9},{5... | collective-permute-start | bytes 196616 | tf_op jit(solution)/shard_map/ppermute | solution.py:100
  222.0 10.0 %collective-permute-start.7 = (bf16[32,1024]{1,0:T(8,128)(2,1)S(1)}, bf16[32,1024]{1,0:T(8,128)(2,1)S(1)}, u32[]{:S(2)}, u32[]{:S(2)}) collective-permute-start(bf16[32,1024]{1,0:T(8,128)(2,1)S(1)} %get-tuple-element.42), channel_id=1, source_target_pairs={{0,16},{4,20},{8,24},{12,28},{16,0},{20,4},{24,8},{28,12},{1,17},{... | collective-permute-start | bytes 196616 | tf_op jit(solution)/shard_map/ppermute | solution.py:100
  222.6 10.2 %collective-permute-start.8 = (bf16[32,1024]{1,0:T(8,128)(2,1)}, bf16[32,1024]{1,0:T(8,128)(2,1)S(1)}, u32[]{:S(2)}, u32[]{:S(2)}) collective-permute-start(bf16[32,1024]{1,0:T(8,128)(2,1)} %get-tuple-element.41), channel_id=1, source_target_pairs={{0,16},{4,20},{8,24},{12,28},{16,0},{20,4},{24,8},{28,12},{1,17},{... | collective-permute-start | bytes 196616 | tf_op jit(solution)/shard_map/ppermute | solution.py:100
  232.8 6.1 %collective-permute-start.11 = (bf16[32,1024]{1,0:T(8,128)(2,1)S(1)}, bf16[32,1024]{1,0:T(8,128)(2,1)S(1)}, u32[]{:S(2)}, u32[]{:S(2)}) collective-permute-start(bf16[32,1024]{1,0:T(8,128)(2,1)S(1)} %get-tuple-element.46), channel_id=1, source_target_pairs={{0,8},{4,12},{8,16},{12,20},{16,24},{20,28},{24,0},{28,4},{1,9},{5... | collective-permute-start | bytes 196616 | tf_op jit(solution)/shard_map/ppermute | solution.py:100
  233.5 6.0 %collective-permute-start.12 = (bf16[32,1024]{1,0:T(8,128)(2,1)S(1)}, bf16[32,1024]{1,0:T(8,128)(2,1)S(1)}, u32[]{:S(2)}, u32[]{:S(2)}) collective-permute-start(bf16[32,1024]{1,0:T(8,128)(2,1)S(1)} %get-tuple-element.45), channel_id=1, source_target_pairs={{0,24},{4,28},{8,0},{12,4},{16,8},{20,12},{24,16},{28,20},{1,25},{... | collective-permute-start | bytes 196616 | tf_op jit(solution)/shard_map/ppermute | solution.py:100
  240.2 12.6 %all-to-all-start.6 = ((bf16[4,2,32,1024]{3,2,1,0:T(8,128)(2,1)}), bf16[4,2,32,1024]{3,2,1,0:T(8,128)(2,1)S(1)}, u32[]{:S(2)}, u32[]{:S(2)}) async-start(bf16[4,2,32,1024]{3,2,1,0:T(8,128)(2,1)} %bitcast_dynamic-update-slice_fusion.8), calls=%async_computation.6 | async-start | bytes 1048576 | tf_op jit(solution)/shard_map/all_to_all | solution.py:141
  (8 other events, 45.5 us)
